TPU v7x, 128 devices: a whole 4x4x4 slice. The times are simulated.
128 devices in a mesh: grp: 4 (over y), sub: 32 (over x, z, core).
Axes of the slice: x: 4, y: 4, z: 4, core: 2. Of those that a mesh axis runs over, the one named last changes fastest.
Arguments:
- basis_cols: bfloat16 [128, 1024, 32, 128], P('grp', 'sub'), may hold values from -0.375 to 0.375
- diag_weight: float32 [128, 1024, 32], P('grp', 'sub'), may hold values from 0.5 to 4
- link_weight: float32 [128, 1024, 32], P('grp', 'sub'), may hold values from 0.3 to 1
- base_front: bfloat16 [16384, 16384], P('grp', 'sub'), may hold values from -4 to 4
- block_lists: int32 [16384, 2], replicated, may hold values from 0 to 127, as said below
Outputs:
- trailing: float32 [16384, 16384], P('grp', 'sub')
- panel_factor: bfloat16 [16384, 512], P(('grp', 'sub'))
Inputs may be any that keep to these rules, and one draw needn't show every extreme that they name: `block_lists`: rows follow the tiles' numbering. Every row block is at least its column block, and row block times 128 is at least 512. Block (a, b) is held by the device (a // 32, b // 4) of the mesh; at most 2 tiles of one subdomain go to blocks held by one device, and in every draw some subdomain sends exactly 2 to one device.
All inputs are finite; a program needn't handle non-finite values.
Results may differ from a plain program's by a relative error of at most 0.0039.
Values may be sent and summed in bfloat16 or wider, within the bound.
A program may use at most 192 MiB of HBM per device.

v0:
```python
import jax
import jax.numpy as jnp
from jax import lax
from jax.sharding import PartitionSpec as P

TILES_DEV = 128


def extended_2(x, sides, width):
    for axis, dim in sides:
        count, length = (lax.axis_size(axis), x.shape[dim])
        up = [(i, (i + 1) % count) for i in range(count - 1)]
        down = [(j, i) for i, j in up]
        last = lax.slice_in_dim(x, length - width, length, axis=dim)
        first = lax.slice_in_dim(x, 0, width, axis=dim)
        before = lax.ppermute(last, axis, up)
        after = lax.ppermute(first, axis, down)
        x = jnp.concatenate([before, x, after], axis=dim)
    return x


def from_root(block, axis, owner):
    block = jnp.where(lax.axis_index(axis) == owner, block, jnp.zeros_like(block))
    return lax.psum(block, axis)


def apply_operator(basis_cols, padded, diag_weight, link_weight):
    lifted = padded.astype(jnp.float32)
    along_x = lifted[:-2] + lifted[1:-1] + lifted[2:]
    along_y = along_x[:, :-2] + along_x[:, 1:-1] + along_x[:, 2:]
    along_z = along_y[:, :, :-2] + along_y[:, :, 1:-1] + along_y[:, :, 2:]
    neighbours = along_z - lifted[1:-1, 1:-1, 1:-1]
    return (
        diag_weight[..., None] * basis_cols.astype(jnp.float32)
        - link_weight[..., None] * neighbours
    )


def pivot_factor(lead_block):
    symmetric = jnp.tril(lead_block) + jnp.tril(lead_block, -1).T
    shifted = symmetric + jnp.diag(jnp.sum(jnp.abs(symmetric), axis=1) + 1.0)
    return jnp.linalg.cholesky(shifted)


def panel_from(front_rows, factor, first_group):
    lower_rows = lax.linalg.triangular_solve(
        factor, front_rows, left_side=False, lower=True, transpose_a=True
    )
    panel_width = factor.shape[0]
    lead_rows = jnp.where(first_group, factor, lower_rows[:panel_width])
    return jnp.concatenate([lead_rows, lower_rows[panel_width:]], axis=0).astype(jnp.bfloat16)


def per_device(basis_cols, diag_weight, link_weight, base_front, block_lists):
    group_count = lax.axis_size("grp")
    member_count = lax.axis_size("sub")
    device_count = group_count * member_count
    group_index = lax.axis_index("grp")
    member_index = lax.axis_index("sub")
    own_index = group_index * member_count + member_index
    basis_width = basis_cols.shape[3]
    panel_width = basis_width * group_count
    row_count = basis_width * member_count
    capacity = 2 * TILES_DEV // device_count
    cell_count = basis_cols.shape[0] * basis_cols.shape[1] * basis_cols.shape[2]
    region_cells = cell_count // TILES_DEV
    scaled = (link_weight[..., None] * basis_cols.astype(jnp.float32)).astype(jnp.bfloat16)
    extended = extended_2(scaled, (("grp", 0), ("sub", 1)), 1)
    padded = jnp.pad(extended, ((0, 0), (0, 0), (1, 1), (0, 0)))
    image_field = apply_operator(basis_cols, padded, diag_weight, link_weight)
    tile_set = jnp.einsum(
        "rck,rcl->rkl",
        basis_cols.reshape(TILES_DEV, region_cells, basis_width).astype(jnp.float32),
        image_field.reshape(TILES_DEV, region_cells, basis_width),
        precision=lax.Precision.HIGHEST,
    )
    listed = block_lists.reshape(device_count, TILES_DEV, 2)
    row_block = listed[:, :, 0]
    col_block = listed[:, :, 1]
    owner_ids = row_block // member_count * member_count + col_block // group_count
    order_ids = jnp.arange(TILES_DEV)
    earlier = order_ids[None, :] < order_ids[:, None]
    slot_rank = jnp.sum((owner_ids[:, :, None] == owner_ids[:, None, :]) & earlier[None], axis=2)
    own_owner = lax.dynamic_index_in_dim(owner_ids, own_index, 0, keepdims=False)
    own_slot = lax.dynamic_index_in_dim(slot_rank, own_index, 0, keepdims=False)
    outgoing = jnp.zeros((device_count, capacity, basis_width, basis_width), jnp.float32)
    outgoing = outgoing.at[own_owner, own_slot].set(tile_set)
    received = lax.all_to_all(outgoing, ("grp", "sub"), split_axis=0, concat_axis=0, tiled=True)
    arriving = owner_ids == own_index
    local_block = row_block % member_count * group_count + col_block % group_count
    sources = jnp.where(arriving, jnp.arange(device_count, dtype=jnp.int32)[:, None], device_count)
    slot_block = jnp.full((device_count, capacity), device_count, jnp.int32)
    slot_block = slot_block.at[sources, slot_rank].set(local_block, mode="drop")
    summed = jax.ops.segment_sum(
        received.reshape(device_count * capacity, basis_width * basis_width),
        slot_block.reshape(-1),
        num_segments=device_count + 1,
    )[:device_count]
    assembled = summed.reshape(member_count, group_count, basis_width, basis_width)
    assembled = assembled.transpose(0, 2, 1, 3).reshape(row_count, panel_width)
    front_local = base_front.astype(jnp.float32) + assembled
    factor = pivot_factor(front_local[:panel_width])
    factor = from_root(factor, "grp", 0)
    first_group = group_index == 0
    panel_local = panel_from(front_local, factor, first_group)
    panel_local = from_root(panel_local, "sub", 0)
    offset = member_index * panel_width % row_count
    source_group = member_index * panel_width // row_count
    piece = lax.dynamic_slice_in_dim(panel_local, offset, panel_width, 0)
    column_rows = from_root(piece, "grp", source_group)
    update = lax.dot_general(
        panel_local, column_rows, (((1,), (1,)), ((), ())), preferred_element_type=jnp.float32
    )
    global_rows = group_index * row_count + jnp.arange(row_count)
    global_cols = member_index * panel_width + jnp.arange(panel_width)
    keep = (global_rows[:, None] >= global_cols[None, :]) & (global_cols[None, :] >= panel_width)
    trailing = jnp.where(keep, front_local - update, 0.0)
    factor_rows = lax.dynamic_slice_in_dim(panel_local, member_index * basis_width, basis_width, 0)
    return (trailing, factor_rows)


def solution(mesh):
    return jax.shard_map(
        per_device,
        mesh=mesh,
        in_specs=(
            P("grp", "sub", None, None),
            P("grp", "sub", None),
            P("grp", "sub", None),
            P("grp", "sub"),
            P(),
        ),
        out_specs=(P("grp", "sub"), P(("grp", "sub"), None)),
        check_vma=False,
    )
```

profile of v0, /device:TPU:121, one launch (start us, length us, event | category | flops | bytes accessed | tf_op | source)
XLA Modules:
  0.0 920.2 jit_solution(7135615745710813139)
XLA Ops:
  7.2 6.4 fusion.2
  13.6 3.4 copy-done.1
  17.0 1.3 collective-permute-start
  18.3 4.0 collective-permute-start.1
  22.7 3.4 collective-permute-done
  26.1 0.9 collective-permute-done.1
  27.0 1.1 pad_maximum_fusion.3
  28.1 3.5 collective-permute-start.2
  31.6 2.2 collective-permute-start.3
  33.8 5.1 convert_reduce_fusion
  38.9 2.6 collective-permute-done.3
  41.6 17.2 %fusion.6 = f32[34,34,34,128]{3,2,1,0:T(8,128)} fusion(bf16[34,1,32,128]{3,2,1,0:T(8,128)(2,1)S(1)} %collective-permute-done.3, bf16[34,1,32,128]{3,2,1,0:T(8,128)(2,1)S(1)} %collective-permute-done.2, bf16[1,32,32,128]{3,2,1,0:T(8,128)(2,1)S(1)} %collective-permute-done.1, bf16[32,32,32,128]{3,2,1,0:T(8,128)(2,1)S(1)} %copy-done.2, ...), kind=kLoop, calls=%fused_computation.23 | loop fusion | flops 90556416 | bytes 29593600 | tf_op jit(solution)/shard_map/convert_element_type | solution.py:28
  58.8 29.8 %slice_add_fusion = f32[32,34,34,128]{3,2,1,0:T(8,128)} fusion(f32[34,34,34,128]{3,2,1,0:T(8,128)} %fusion.6), kind=kLoop, calls=%fused_computation.8 | loop fusion | flops 9469952 | bytes 75759616 | tf_op jit(solution)/shard_map/add | solution.py:29
  88.5 20.8 %slice_add_fusion.2 = f32[32,32,34,128]{3,2,1,0:T(8,128)S(1)} fusion(f32[32,34,34,128]{3,2,1,0:T(8,128)} %slice_add_fusion), kind=kLoop, calls=%fused_computation.12 | loop fusion | flops 8912896 | bytes 71303168 | tf_op jit(solution)/shard_map/add | solution.py:30
  109.4 16.0 %fusion.1 = f32[32,32,32,128]{3,2,1,0:T(8,128)} fusion(bf16[32,32,32,128]{3,2,1,0:T(8,128)(2,1)} %param.5, f32[34,34,34,128]{3,2,1,0:T(8,128)} %fusion.6, f32[32,32,34,128]{3,2,1,0:T(8,128)S(1)} %slice_add_fusion.2, f32[32,32,32]{2,1,0:T(8,128)S(1)} %copy-done.5, f32[32,32,32]{2,1,0:T(8,128)S(1)} %copy-done.6), kind=kLoop, calls=%fused_computation.14 | loop fusion | flops 29360128 | bytes 92536832 | tf_op jit(solution)/shard_map/sub | solution.py:34
  125.4 20.1 %convolution_bitcast_fusion = f32[128,128,128]{1,2,0:T(8,128)} fusion(f32[128,256,128]{2,1,0:T(8,128)} %bitcast.152, bf16[128,256,128]{2,1,0:T(8,128)(2,1)} %bitcast.151), kind=kOutput, calls=%fused_computation.50 | convolution fusion | flops 6442450944 | bytes 33554432 | tf_op jit(solution)/shard_map/rck,rcl->rkl/dot_general | solution.py:71
  145.5 9.2 %copy.54 = f32[128,128,128]{2,1,0:T(8,128)} copy(f32[128,128,128]{1,2,0:T(8,128)} %convolution_bitcast_fusion) | data formatting | bytes 16777216 | tf_op jit(solution)/shard_map/rck,rcl->rkl/dot_general | solution.py:71
  154.7 7.8 broadcast_in_dim.79
  162.6 24.7 %scatter_fusion = f32[128,2,128,128]{3,2,1,0:T(8,128)} fusion(f32[128,2,128,128]{3,2,1,0:T(8,128)} %broadcast_in_dim.79, s32[128]{0:T(128)S(1)} %fusion.69, f32[128,128,128]{2,1,0:T(8,128)} %copy.54), kind=kCustom, calls=%fused_computation | custom fusion | bytes 25166848 | tf_op jit(solution)/shard_map/scatter | solution.py:87
  187.3 11.3 %all-to-all-start = ((f32[128,2,128,128]{3,2,1,0:T(8,128)}), f32[128,2,128,128]{3,2,1,0:T(8,128)}, u32[]{:S(2)}, u32[]{:S(2)}) async-start(f32[128,2,128,128]{3,2,1,0:T(8,128)} %scatter_fusion), calls=%async_computation | async-start | bytes 33554432 | tf_op jit(solution)/shard_map/all_to_all | solution.py:88
  198.9 60.3 %scatter_custom_fusion.2 = s32[256]{0:T(256)S(1)} fusion(s32[16384]{0:T(1024)S(1)} %select_bitcast_fusion, s32[16384]{0:T(1024)S(1)} %get-tuple-element.42, s32[]{:T(128)} %constant.242.clone.1), kind=kCustom, calls=%fused_computation.177 | custom fusion | bytes 1028
  259.5 152.7 %all-to-all-done = f32[128,2,128,128]{3,2,1,0:T(8,128)} async-done(((f32[128,2,128,128]{3,2,1,0:T(8,128)}), f32[128,2,128,128]{3,2,1,0:T(8,128)}, u32[]{:S(2)}, u32[]{:S(2)}) %all-to-all-start) | async-done | bytes 16777248 | tf_op jit(solution)/shard_map/all_to_all | solution.py:88
  412.2 18.4 %copy.79 = f32[32,8,128,128]{3,1,2,0:T(8,128)} copy(f32[32,8,128,128]{3,2,1,0:T(8,128)} %bitcast.36) | data formatting | bytes 33554432
  430.6 42.6 %scatter_custom_fusion.1 = f32[129,16384]{1,0:T(8,128)} fusion(s32[256]{0:T(256)S(1)} %reshape.254, f32[32,8,128,128]{3,1,2,0:T(8,128)} %copy.79, f32[]{:T(128)} %constant.241.clone.1), kind=kCustom, calls=%fused_computation.16 | custom fusion | flops 4194304 | bytes 25231364 | tf_op jit(solution)/shard_map/scatter-add | solution.py:94
  473.3 4.0 slice_bitcast_fusion
  477.3 4.9 copy.80
  482.1 13.9 %copy.55 = f32[32,128,4,128]{3,2,1,0:T(4,128)} copy(f32[32,128,4,128]{3,1,2,0:T(8,128)} %bitcast.153) | data formatting | bytes 16777216 | tf_op jit(solution)/shard_map/transpose | solution.py:100
  496.1 5.0 bitcast_add_fusion
  501.1 3.4 copy-done
  504.9 1.5 abs_reduce_fusion
  506.4 1.6 select_add_fusion
  508.6 11.7 %cholesky.103 = f32[128,128]{1,0:T(8,128)S(1)} custom-call(f32[128,128]{1,0:T(8,128)S(1)} %cholesky.263), custom_call_target="Cholesky" | custom-call | tf_op jit(solution)/shard_map/jit(cholesky)/cholesky | solution.py:42
  520.4 9.8 %custom-call.30 = f32[1,128,128]{1,2,0:T(8,128)S(1)} custom-call(f32[1,128,128]{2,1,0:T(8,128)S(1)} %get-tuple-element.58), custom_call_target="InvertDiagBlocksLowerTriangular" | custom-call | tf_op jit(solution)/shard_map/jit(cholesky)/cholesky | solution.py:42
  530.9 11.7 %cholesky.215 = f32[128,128]{1,0:T(8,128)S(1)} custom-call(f32[128,128]{1,0:T(8,128)S(1)} %cholesky.267), custom_call_target="Cholesky" | custom-call | tf_op jit(solution)/shard_map/jit(cholesky)/cholesky | solution.py:42
  543.1 10.2 %custom-call.31 = f32[1,128,128]{1,2,0:T(8,128)S(1)} custom-call(f32[1,128,128]{2,1,0:T(8,128)S(1)} %get-tuple-element.56), custom_call_target="InvertDiagBlocksLowerTriangular" | custom-call | tf_op jit(solution)/shard_map/jit(cholesky)/cholesky | solution.py:42
  554.2 11.7 %cholesky.236 = f32[128,128]{1,0:T(8,128)S(1)} custom-call(f32[128,128]{1,0:T(8,128)S(1)} %cholesky.272), custom_call_target="Cholesky" | custom-call | tf_op jit(solution)/shard_map/jit(cholesky)/cholesky | solution.py:42
  566.1 9.8 %custom-call.32 = f32[1,128,128]{1,2,0:T(8,128)S(1)} custom-call(f32[1,128,128]{2,1,0:T(8,128)S(1)} %get-tuple-element.54), custom_call_target="InvertDiagBlocksLowerTriangular" | custom-call | tf_op jit(solution)/shard_map/jit(cholesky)/cholesky | solution.py:42
  576.7 11.8 %cholesky.253 = f32[128,128]{1,0:T(8,128)S(1)} custom-call(f32[128,128]{1,0:T(8,128)S(1)} %convolution_subtract_fusion.4), custom_call_target="Cholesky" | custom-call | tf_op jit(solution)/shard_map/jit(cholesky)/cholesky | solution.py:42
  588.7 0.7 compare_reduce_fusion.1
  590.0 0.7 compare_reduce_fusion.2
  593.2 1.2 select_select_fusion
  594.5 63.1 %all-reduce.6.cloned.1.call-done = f32[512,512]{0,1:T(8,128)} async-done(((f32[512,512]{0,1:T(8,128)}), f32[512,512]{0,1:T(8,128)}) %all-reduce.6.cloned.1.call-update) | async-done | bytes 1048592 | tf_op jit(solution)/shard_map/psum | solution.py:24
  657.6 1.3 fusion.29
  658.9 8.6 while.1
  659.6 1.3 dynamic-slice.7
  661.8 1.3 dynamic-slice.7
  663.9 1.3 dynamic-slice.7
  666.1 1.3 dynamic-slice.7
  667.5 39.3 %custom-call.33 = f32[4,128,128]{1,2,0:T(8,128)S(1)} custom-call(f32[4,128,128]{2,1,0:T(8,128)S(1)} %get-tuple-element.9), custom_call_target="InvertDiagBlocksLowerTriangular" | custom-call | tf_op jit(solution)/shard_map/triangular_solve | solution.py:46
  706.9 3.6 fusion.25
  710.5 5.2 convolution_subtract_fusion.1
  715.6 2.1 fusion.49
  717.7 9.1 convolution_subtract_fusion
  726.8 2.0 fusion.48
  728.8 12.8 %fusion.18 = f32[4096,128]{1,0:T(8,128)S(1)} fusion(f32[4096,128]{0,1:T(8,128)S(1)} %fusion.48, f32[4096,128]{0,1:T(8,128)S(1)} %fusion.49, f32[4096,128]{0,1:T(8,128)S(1)} %fusion.25, f32[4096,512]{1,0:T(8,128)} %copy-done, f32[512,512]{0,1:T(8,128)S(1)} %get-tuple-element.116), kind=kOutput, calls=%fused_computation.44 | convolution fusion | flops 2419589120 | bytes 10682368 | tf_op jit(solution)/shard_map/triangular_solve | solution.py:46
  741.6 2.0 fusion.47
  743.6 0.8 pad_maximum_fusion
  745.0 2.4 maximum_select_fusion
  747.6 113.9 %all-reduce.8.cloned.1.call-done = bf16[4096,512]{0,1:T(8,128)(2,1)} async-done(((bf16[4096,512]{0,1:T(8,128)(2,1)}), bf16[4096,512]{0,1:T(8,128)(2,1)}) %all-reduce.8.cloned.1.call-update) | async-done | bytes 4194320 | tf_op jit(solution)/shard_map/psum | solution.py:24
  861.5 1.9 dynamic-slice_select_fusion
  863.5 0.9 constant_dynamic-slice_fusion.1
  864.4 0.8 copy.67
  865.2 39.6 %all-reduce.10.cloned.1.call-done = bf16[512,512]{0,1:T(8,128)(2,1)} async-done(((bf16[512,512]{0,1:T(8,128)(2,1)}), bf16[512,512]{0,1:T(8,128)(2,1)}) %all-reduce.10.cloned.1.call-update) | async-done | bytes 524304 | tf_op jit(solution)/shard_map/psum | solution.py:24
  904.8 8.4 subtract_select_fusion
  (92 shorter events, 9.5 us)
Async XLA Ops:
  7.2 15.2 %copy-start.7 = (s32[16384,2]{0,1:T(2,128)S(1)}, s32[16384,2]{0,1:T(2,128)}, u32[]{:S(2)}) copy-start(s32[16384,2]{0,1:T(2,128)} %param.9) | copy-start | bytes 393220
  13.6 3.4 copy-start.1
  17.0 9.1 collective-permute-start
  18.3 8.6 collective-permute-start.1
  22.6 19.0 %copy-start.2 = (bf16[32,32,32,128]{3,2,1,0:T(8,128)(2,1)S(1)}, bf16[32,32,32,128]{3,2,1,0:T(8,128)(2,1)}, u32[]{:S(2)}) copy-start(bf16[32,32,32,128]{3,2,1,0:T(8,128)(2,1)} %copy-done.1) | copy-start | bytes 25165828
  28.1 10.9 %collective-permute-start.2 = (bf16[34,1,32,128]{3,2,1,0:T(8,128)(2,1)S(1)}, bf16[34,1,32,128]{3,2,1,0:T(8,128)(2,1)S(1)}, u32[]{:S(2)}, u32[]{:S(2)}) collective-permute-start(bf16[34,1,32,128]{3,2,1,0:T(8,128)(2,1)S(1)} %get-tuple-element.49), channel_id=1, source_target_pairs={{0,1},{1,2},{2,3},{3,4},{4,5},{5,6},{6,7},{7,8},{8,9},{9,10},{10,1... | collective-permute-start | bytes 835592 | tf_op jit(solution)/shard_map/ppermute | solution.py:16
  31.6 10.0 %collective-permute-start.3 = (bf16[34,1,32,128]{3,2,1,0:T(8,128)(2,1)S(1)}, bf16[34,1,32,128]{3,2,1,0:T(8,128)(2,1)S(1)}, u32[]{:S(2)}, u32[]{:S(2)}) collective-permute-start(bf16[34,1,32,128]{3,2,1,0:T(8,128)(2,1)S(1)} %get-tuple-element.50), channel_id=1, source_target_pairs={{1,0},{2,1},{3,2},{4,3},{5,4},{6,5},{7,6},{8,7},{9,8},{10,9},{11,1... | collective-permute-start | bytes 835592 | tf_op jit(solution)/shard_map/ppermute | solution.py:17
  88.5 20.8 %copy-start.5 = (f32[32,32,32]{2,1,0:T(8,128)S(1)}, f32[32,32,32]{2,1,0:T(8,128)}, u32[]{:S(2)}) copy-start(f32[32,32,32]{2,1,0:T(8,128)} %param.7) | copy-start | bytes 393220
  88.5 20.8 %copy-start.6 = (f32[32,32,32]{2,1,0:T(8,128)S(1)}, f32[32,32,32]{2,1,0:T(8,128)}, u32[]{:S(2)}) copy-start(f32[32,32,32]{2,1,0:T(8,128)} %param.6) | copy-start | bytes 393220
  187.3 11.4 %copy-start.9 = (s32[2]{0:T(128)S(1)}, s32[2]{0:T(128)}, u32[]{:S(2)}) copy-start(s32[2]{0:T(128)} %constant.265) | copy-start | bytes 28
  187.3 11.5 %copy-start.8 = (s32[2]{0:T(128)S(1)}, s32[2]{0:T(128)}, u32[]{:S(2)}) copy-start(s32[2]{0:T(128)} %constant.268) | copy-start | bytes 28
  187.3 224.9 %all-to-all-start = ((f32[128,2,128,128]{3,2,1,0:T(8,128)}), f32[128,2,128,128]{3,2,1,0:T(8,128)}, u32[]{:S(2)}, u32[]{:S(2)}) async-start(f32[128,2,128,128]{3,2,1,0:T(8,128)} %scatter_fusion), calls=%async_computation | async-start | bytes 33554432 | tf_op jit(solution)/shard_map/all_to_all | solution.py:88
  198.6 459.0 %all-reduce.6.cloned.1.call-start = ((), (), s32[]{:S(2)}) async-start(), calls=%async_computation.1 | async-start | bytes 2097152 | tf_op jit(solution)/shard_map/psum | solution.py:24
  482.1 13.9 %copy-start.3 = (bf16[4096,512]{1,0:T(8,128)(2,1)S(1)}, bf16[4096,512]{1,0:T(8,128)(2,1)}, u32[]{:S(2)}) copy-start(bf16[4096,512]{1,0:T(8,128)(2,1)} %param.8) | copy-start | bytes 12582916
  501.0 3.4 copy-start
  594.4 267.0 %all-reduce.8.cloned.1.call-start = ((), (), s32[]{:S(2)}) async-start(), calls=%async_computation.2 | async-start | bytes 8388608 | tf_op jit(solution)/shard_map/psum | solution.py:24
  743.6 1.2 copy-start.4
  747.5 157.3 %all-reduce.10.cloned.1.call-start = ((), (), s32[]{:S(2)}) async-start(), calls=%async_computation.3 | async-start | bytes 1048576 | tf_op jit(solution)/shard_map/psum | solution.py:24
Sparse Core Ops, SparseCore 0:
  594.6 62.9 all-reduce.5
  747.6 113.8 all-reduce.7
  863.9 40.7 all-reduce.9
where the time goes:
time: 935 us; the launch traced here: 920 us
  waiting for transfers between devices  376 us (40%)
  other arithmetic  274 us (29%)
  local copies, waits for them, and re-layouts  162 us (17%)
  matrix products  67.6 us (7%)
  starting transfers between devices  22.4 us (2%)
  between operations  17.4 us (2%)
    psum x3, waiting for transfers between devices, from_root(): return lax.psum(block, axis)  217 us
    all_to_all x1, waiting for transfers between devices, per_device(): lax.all_to_all(outgoing, ('grp', 'sub'), split_axis=0, concat_axis=0, til...  153 us
    unnamed x26, local copies, waits for them, and re-layouts  95.3 us
    another operation x14, other arithmetic, pivot_factor(): return jnp.linalg.cholesky(shifted)  78.9 us
    scatter-add x1, other arithmetic, per_device(): jax.ops.segment_sum(received.reshape(device_count * capacity, basis_width...  42.6 us
    another operation x4, other arithmetic, panel_from(): lax.linalg.triangular_solve(factor, front_rows, left_side=False, lower=Tr...  41.4 us
    another operation x7, matrix products, panel_from(): lax.linalg.triangular_solve(factor, front_rows, left_side=False, lower=Tr...  36.7 us
    add x1, other arithmetic, apply_operator(): along_x = lifted[:-2] + lifted[1:-1] + lifted[2:]  29.8 us
  transfers between devices with their start and end apart: 8, of which 7 were waited for; matrix products, arithmetic and copies ran while one was open for 7% of the time, Pallas kernels for 0%

commit v1 on v0

v1 whole, which is shorter than its diff:
```python
import functools

import jax
import jax.numpy as jnp
from jax import lax
from jax.experimental import pallas as pl
from jax.experimental.pallas import tpu as pltpu
from jax.sharding import PartitionSpec as P

NT = (((1,), (1,)), ((), ()))
NN = (((1,), (0,)), ((), ()))
BF = jnp.bfloat16
F32 = jnp.float32


def dot32(a, b, dims):
    return lax.dot_general(a, b, dims, precision=lax.Precision.HIGHEST, preferred_element_type=F32)


def dotb(a, b, dims):
    return lax.dot_general(a, b, dims, preferred_element_type=F32)


def tile_kernel(
    slot_ref, basis_ref, link_next_ref, link_ref, diag_ref, before_y_ref, after_y_ref,
    before_x_ref, after_x_ref, stencil_ref, eye_ref, out_ref,
    scaled_t, basis_t, partial, stage, sems,
):
    step = pl.program_id(0)
    steps = pl.num_programs(0)
    here = lax.rem(step, 2)
    there = lax.rem(step + 1, 2)
    eye = eye_ref[...]
    gap = jnp.zeros((96, 128), BF)
    first = jnp.concatenate([gap, before_y_ref[0]], axis=0)
    last = jnp.concatenate([after_y_ref[0], gap], axis=0)
    scaled_t[here, :, 0:128] = dotb(eye, first, NT).astype(BF)
    scaled_t[here, :, 1152:1280] = dotb(eye, last, NT).astype(BF)

    @pl.when((step > 0) & (step < steps - 1))
    def _():
        turned = dotb(eye, basis_ref[0], NT)
        basis_t[here] = turned.astype(BF)
        scaled_t[here, :, 128:1152] = (turned * link_next_ref[0]).astype(BF)

    @pl.when(step == 0)
    def _():
        scaled_t[here, :, 128:1152] = dotb(eye, before_x_ref[...], NT).astype(BF)

    @pl.when(step == steps - 1)
    def _():
        scaled_t[here, :, 128:1152] = dotb(eye, after_x_ref[...], NT).astype(BF)

    ring = lax.rem(step, 3)
    for q in range(4):
        partial[ring, :, 256 * q:256 * q + 256] = dotb(
            scaled_t[here, :, 256 * q:256 * q + 512], stencil_ref[...], NN
        )

    def copy_out(buffer, q, slot):
        return pltpu.make_async_copy(stage.at[buffer, q], out_ref.at[slot], sems.at[buffer, q])

    @pl.when(step >= 2)
    def _():
        @pl.when(step >= 4)
        def _():
            for q in range(4):
                copy_out(here, q, 0).wait()

        for q in range(4):
            cells = slice(256 * q, 256 * q + 256)
            around = partial[0, :, cells] + partial[1, :, cells] + partial[2, :, cells]
            around = around - scaled_t[there, :, 128 + 256 * q:384 + 256 * q].astype(F32)
            own = basis_t[there, :, cells]
            image = diag_ref[0, :, cells] * own.astype(F32) - link_ref[0, :, cells] * around
            high = image.astype(BF)
            low = (image - high.astype(F32)).astype(BF)
            stage[here, q] = (dotb(own, high, NT) + dotb(own, low, NT)).astype(BF)
            copy_out(here, q, slot_ref[(step - 2) * 4 + q]).start()

    @pl.when(step == steps - 1)
    def _():
        for q in range(4):
            copy_out(there, q, 0).wait()
            copy_out(here, q, 0).wait()


def galerkin_tiles(slots, basis, link, diag, before_y, after_y, before_x, after_x):
    planes = basis.shape[0]
    k = jnp.arange(512)[:, None]
    n = jnp.arange(256)[None, :]
    stencil = (
        (jnp.abs(k // 32 - 4 - n // 32) <= 1) & (jnp.abs(k % 32 - n % 32) <= 1)
    ).astype(BF)
    eye = jnp.eye(128, dtype=BF)
    ahead = lambda t, s: (jnp.clip(t - 1, 0, planes - 1), 0, 0)
    done = lambda t, s: (jnp.clip(t - 2, 0, planes - 1), 0, 0)
    each = lambda t, s: (t, 0, 0)
    whole = lambda t, s: (0, 0)
    return pl.pallas_call(
        tile_kernel,
        out_shape=jax.ShapeDtypeStruct((256, 128, 128), BF),
        grid_spec=pltpu.PrefetchScalarGridSpec(
            num_scalar_prefetch=1,
            grid=(planes + 2,),
            in_specs=[
                pl.BlockSpec((1, 1024, 128), ahead),
                pl.BlockSpec((1, 1, 1024), ahead),
                pl.BlockSpec((1, 1, 1024), done),
                pl.BlockSpec((1, 1, 1024), done),
                pl.BlockSpec((1, 32, 128), each),
                pl.BlockSpec((1, 32, 128), each),
                pl.BlockSpec((1024, 128), whole),
                pl.BlockSpec((1024, 128), whole),
                pl.BlockSpec((512, 256), whole),
                pl.BlockSpec((128, 128), whole),
            ],
            out_specs=pl.BlockSpec(memory_space=pl.ANY),
            scratch_shapes=[
                pltpu.VMEM((2, 128, 1280), BF),
                pltpu.VMEM((2, 128, 1024), BF),
                pltpu.VMEM((3, 128, 1024), F32),
                pltpu.VMEM((2, 4, 128, 128), BF),
                pltpu.SemaphoreType.DMA((2, 4)),
            ],
        ),
        compiler_params=pltpu.CompilerParams(
            dimension_semantics=("arbitrary",), vmem_limit_bytes=32 * 2**20
        ),
        name="galerkin_tiles",
    )(slots, basis, link, link, diag, before_y, after_y, before_x, after_x, stencil, eye)


def factor_kernel(pivot_ref, factor_ref, inverse_ref, work, block):
    size = pivot_ref.shape[0]
    count = size // 128
    rows = lax.broadcasted_iota(jnp.int32, (128, 128), 0)
    lanes = lax.broadcasted_iota(jnp.int32, (128, 128), 1)
    row_ids = lax.broadcasted_iota(jnp.int32, (128, 1), 0)
    lane_ids = lax.broadcasted_iota(jnp.int32, (1, 128), 1)
    work[...] = pivot_ref[...]
    factor_ref[...] = jnp.zeros_like(factor_ref)
    inverse_ref[...] = jnp.zeros_like(inverse_ref)
    for b in range(count):
        own = slice(128 * b, 128 * b + 128)
        rest = slice(128 * b + 128, size)
        block[:, 0:128] = work[own, own]
        block[:, 128:256] = jnp.where(rows == lanes, 1.0, 0.0)

        def eliminate(j, carry):
            left = block[:, 0:128]
            right = block[:, 128:256]
            pivot_row = block[pl.ds(j, 1), :]
            pivot = jnp.sum(jnp.where(lane_ids == j, pivot_row[:, 0:128], 0.0), axis=1, keepdims=True)
            column = jnp.sum(jnp.where(lanes == j, left, 0.0), axis=1, keepdims=True)
            ratio = jnp.where(row_ids > j, column * (1.0 / pivot), 0.0)
            block[:, 0:128] = left - ratio * pivot_row[:, 0:128]
            block[:, 128:256] = right - ratio * pivot_row[:, 128:256]
            return carry

        lax.fori_loop(0, 128, eliminate, 0)
        upper = block[:, 0:128]
        pivots = jnp.sum(jnp.where(rows == lanes, upper, 0.0), axis=1, keepdims=True)
        scale = 1.0 / jnp.sqrt(pivots)
        upper = jnp.where(rows <= lanes, upper * scale, 0.0)
        inverse = jnp.where(rows >= lanes, block[:, 128:256] * scale, 0.0)
        factor_ref[own, own] = upper.T
        inverse_ref[own, own] = inverse
        if b + 1 < count:
            below = dot32(work[rest, own], inverse, NT)
            factor_ref[rest, own] = below
            work[rest, rest] = work[rest, rest] - dot32(below, below, NT)
    for b in range(1, count):
        own = slice(128 * b, 128 * b + 128)
        left = slice(0, 128 * b)
        product = dot32(factor_ref[own, left], inverse_ref[left, left], NN)
        inverse_ref[own, left] = -dot32(inverse_ref[own, own], product, NN)


def pivot_factor(pivot_matrix):
    size = pivot_matrix.shape[0]
    return pl.pallas_call(
        factor_kernel,
        out_shape=[jax.ShapeDtypeStruct((size, size), F32)] * 2,
        in_specs=[pl.BlockSpec(memory_space=pltpu.VMEM)],
        out_specs=[pl.BlockSpec(memory_space=pltpu.VMEM)] * 2,
        scratch_shapes=[pltpu.VMEM((size, size), F32), pltpu.VMEM((128, 256), F32)],
        compiler_params=pltpu.CompilerParams(vmem_limit_bytes=32 * 2**20),
        cost_estimate=pl.CostEstimate(flops=10**10, bytes_accessed=3 * 2**20, transcendentals=0),
        name="pivot_factor",
    )(pivot_matrix)


def final_kernel(place_ref, row_ref, col_ref, base_ref, received_ref, out_ref, sums):
    step = pl.program_id(0)
    group = lax.axis_index("grp")
    member = lax.axis_index("sub")
    row_start = group * 4096
    col_start = member * 512
    live = (member > 0) & (row_start + 4095 >= col_start)

    @pl.when(live & (step == 0))
    def _():
        sums[...] = jnp.zeros_like(sums)

        def add(slot, carry):
            place = place_ref[slot]

            @pl.when(place >= 0)
            def _():
                sums[place] = sums[place] + received_ref[slot].astype(F32)

            return carry

        lax.fori_loop(0, 256, add, 0)

    first_row = row_start + step * 512

    @pl.when(live & (first_row + 511 >= col_start))
    def _():
        update = dotb(row_ref[...], col_ref[...], NT)
        rows = first_row + lax.broadcasted_iota(jnp.int32, (128, 128), 0)
        cols = col_start + lax.broadcasted_iota(jnp.int32, (128, 128), 1)
        for i in range(4):
            for j in range(4):
                r = slice(128 * i, 128 * i + 128)
                c = slice(128 * j, 128 * j + 128)
                value = base_ref[r, c].astype(F32) + sums[(step * 4 + i) * 4 + j] - update[r, c]
                out_ref[r, c] = jnp.where(rows + 128 * i >= cols + 128 * j, value, 0.0)

    @pl.when(jnp.logical_not(live & (first_row + 511 >= col_start)))
    def _():
        out_ref[...] = jnp.zeros_like(out_ref)


def trailing_front(place, panel_rows, panel_cols, base, received):
    return pl.pallas_call(
        final_kernel,
        out_shape=jax.ShapeDtypeStruct((4096, 512), F32),
        grid_spec=pltpu.PrefetchScalarGridSpec(
            num_scalar_prefetch=1,
            grid=(8,),
            in_specs=[
                pl.BlockSpec((512, 512), lambda t, s: (t, 0)),
                pl.BlockSpec((512, 512), lambda t, s: (0, 0)),
                pl.BlockSpec((512, 512), lambda t, s: (t, 0)),
                pl.BlockSpec((256, 128, 128), lambda t, s: (0, 0, 0)),
            ],
            out_specs=pl.BlockSpec((512, 512), lambda t, s: (t, 0)),
            scratch_shapes=[pltpu.VMEM((128, 128, 128), F32)],
        ),
        compiler_params=pltpu.CompilerParams(
            dimension_semantics=("arbitrary",), vmem_limit_bytes=48 * 2**20
        ),
        name="trailing_front",
    )(place, panel_rows, panel_cols, base, received)


def shifted(x, axis, count, up):
    pairs = [(i, i + 1) if up else (i + 1, i) for i in range(count - 1)]
    return lax.ppermute(x, axis, pairs)


def arrivals(owner_ids, local_block, owner):
    order = jnp.arange(owner_ids.shape[1], dtype=jnp.int32)[None, :]
    here = owner_ids == owner
    first = jnp.min(jnp.where(here, order, 1 << 20), axis=1, keepdims=True)
    one = jnp.max(jnp.where(here & (order == first), local_block, -1), axis=1)
    two = jnp.max(jnp.where(here & (order > first), local_block, -1), axis=1)
    return jnp.stack([one, two], axis=1).reshape(-1)


def per_device(basis_cols, diag_weight, link_weight, base_front, block_lists):
    groups, members, devices = 4, 32, 128
    group = lax.axis_index("grp")
    member = lax.axis_index("sub")
    me = group * members + member

    lead = jnp.where(me == 0, base_front[:512], jnp.zeros((512, 512), BF))
    lead = lax.psum(lead, ("grp", "sub"))
    base_rows = lax.all_to_all(
        base_front.reshape(members, 128, 512), "sub", split_axis=0, concat_axis=0, tiled=True
    )[0]

    def scaled(b, w):
        return (w[..., None] * b.astype(F32)).astype(BF)

    before_x = shifted(scaled(basis_cols[31], link_weight[31]), "grp", groups, True)
    after_x = shifted(scaled(basis_cols[0], link_weight[0]), "grp", groups, False)
    high_y = scaled(basis_cols[:, 31], link_weight[:, 31])
    low_y = scaled(basis_cols[:, 0], link_weight[:, 0])
    high_y = jnp.concatenate([before_x[None, 31], high_y, after_x[None, 31]], axis=0)
    low_y = jnp.concatenate([before_x[None, 0], low_y, after_x[None, 0]], axis=0)
    before_y = shifted(high_y, "sub", members, True)
    after_y = shifted(low_y, "sub", members, False)

    listed = block_lists.reshape(devices, 128, 2)
    row_block = listed[:, :, 0]
    col_block = listed[:, :, 1]
    owner_ids = row_block // members * members + col_block // groups
    local_block = row_block % members * groups + col_block % groups
    own_owner = lax.dynamic_index_in_dim(owner_ids, me, 0, keepdims=False)
    order = jnp.arange(128)
    rank = jnp.sum(
        (own_owner[:, None] == own_owner[None, :]) & (order[None, :] < order[:, None]), axis=1
    )
    slots = (own_owner * 2 + rank).astype(jnp.int32)
    place = arrivals(owner_ids, local_block, me)
    panel_place = arrivals(owner_ids, local_block, group * members)

    outgoing = galerkin_tiles(
        slots,
        basis_cols.reshape(32, 1024, 128),
        link_weight.reshape(32, 1, 1024),
        diag_weight.reshape(32, 1, 1024),
        before_y,
        after_y,
        before_x.reshape(1024, 128),
        after_x.reshape(1024, 128),
    )

    strips = outgoing.reshape(groups, members, 2, 128, 128)[:, 0]
    strips = strips.reshape(groups, 2, members, 4, 128).transpose(0, 2, 1, 3, 4)
    strips = strips.reshape(devices, 2, 4, 128)
    strips = lax.all_to_all(strips, ("grp", "sub"), split_axis=0, concat_axis=0, tiled=True)
    strips, outgoing = lax.optimization_barrier((strips, outgoing))
    received = lax.all_to_all(
        outgoing.reshape(devices, 2, 128, 128), ("grp", "sub"), split_axis=0, concat_axis=0, tiled=True
    ).reshape(256, 128, 128)

    strips = jnp.where((panel_place >= 0)[:, None], strips.reshape(256, 512), 0)
    pick = (panel_place[None, :] == jnp.arange(128)[:, None]).astype(BF)
    strips = dotb(pick, strips, NN).reshape(members, groups, 4, 128)
    strips = strips.transpose(0, 2, 1, 3).reshape(members, 4, 512)
    strips = lax.all_to_all(strips, "sub", split_axis=0, concat_axis=0, tiled=True)
    front_rows = base_rows.astype(F32) + strips.reshape(128, 512)

    lead = lead.astype(F32)
    symmetric = jnp.tril(lead) + jnp.tril(lead, -1).T
    pivot_matrix = symmetric + jnp.diag(jnp.sum(jnp.abs(symmetric), axis=1) + 1.0)
    factor, inverse = pivot_factor(pivot_matrix)
    solved = dot32(front_rows, inverse, NT)
    in_lead = (group == 0) & (member < 4)
    own_factor = lax.dynamic_slice_in_dim(factor, 128 * jnp.minimum(member, 3), 128, 0)
    panel = jnp.where(in_lead, own_factor, solved).astype(BF)
    panel_rows = lax.all_gather(panel, "sub", axis=0, tiled=True)

    source = member // 8
    piece = lax.dynamic_slice_in_dim(panel_rows, member % 8 * 512, 512, 0)
    panel_cols = jnp.where(group == source, piece, jnp.zeros_like(piece))
    total = panel_cols
    for ahead in range(1, groups):
        pairs = [
            (s // 8 * members + s, (s // 8 + ahead) * members + s)
            for s in range(members)
            if s // 8 + ahead < groups
        ]
        total = total + lax.ppermute(panel_cols, ("grp", "sub"), pairs)
    trailing = trailing_front(place, panel_rows, total, base_front, received)
    return (trailing, panel)


def solution(mesh):
    return jax.shard_map(
        per_device,
        mesh=mesh,
        in_specs=(
            P("grp", "sub", None, None),
            P("grp", "sub", None),
            P("grp", "sub", None),
            P("grp", "sub"),
            P(),
        ),
        out_specs=(P("grp", "sub"), P(("grp", "sub"), None)),
        check_vma=False,
    )
```

time: 935 us -> 569 us (0.61)
  the two profiles are of different devices: /device:TPU:121 before, /device:TPU:9 now
where the time goes in v1:
time: 569 us; the launch traced here: 568 us
  waiting for transfers between devices  337 us (59%)
  Pallas kernels  136 us (24%)
  starting transfers between devices  38.8 us (7%)
  local copies, waits for them, and re-layouts  15.8 us (3%)
  between operations  14.5 us (3%)
  blocking collectives  13.4 us (2%)
  other arithmetic  10.1 us (2%)
    psum x1, waiting for transfers between devices, per_device(): lead = lax.psum(lead, ('grp', 'sub'))  171 us
    all_gather x1, waiting for transfers between devices, per_device(): panel_rows = lax.all_gather(panel, 'sub', axis=0, tiled=True)  121 us
    pallas_call x1, Pallas kernels, galerkin_tiles(): pl.pallas_call(tile_kernel, out_shape=jax.ShapeDtypeStruct((256, 128, 128...  59.7 us
    pallas_call x1, Pallas kernels, pivot_factor(): pl.pallas_call(factor_kernel, out_shape=[jax.ShapeDtypeStruct((size, size...  59.4 us
    ppermute x3, waiting for transfers between devices, per_device(): total = total + lax.ppermute(panel_cols, ('grp', 'sub'), pairs)  26 us
    pallas_call x1, Pallas kernels, trailing_front(): pl.pallas_call(final_kernel, out_shape=jax.ShapeDtypeStruct((4096, 512),...  17.1 us
    all_to_all x1, blocking collectives, per_device(): lax.all_to_all(strips, 'sub', split_axis=0, concat_axis=0, tiled=True)  13.4 us
    ppermute x4, starting transfers between devices, shifted(): return lax.ppermute(x, axis, pairs)  12.7 us
  transfers between devices with their start and end apart: 12, of which 8 were waited for; matrix products, arithmetic and copies ran while one was open for 2% of the time, Pallas kernels for 10%

profile of v1, /device:TPU:9, one launch (start us, length us, event | category | flops | bytes accessed | tf_op | source)
XLA Modules:
  0.0 568.4 jit_solution(16015223610843121873)
XLA Ops:
  7.2 0.0 copy-start.3
  7.2 1.1 fusion.42
  8.3 0.7 slice_bitcast_fusion.5
  9.0 1.8 fusion.1
  10.8 1.9 collective-permute-start.1
  12.8 3.4 collective-permute-start
  16.2 0.9 copy.73
  17.1 0.2 select_reduce_fusion.5
  17.3 0.1 select_reduce_fusion.2
  17.4 0.2 convert_reduce_fusion
  17.6 0.2 select_reduce_fusion.1
  17.9 2.1 collective-permute-done.1
  19.9 1.5 collective-permute-done
  21.5 5.5 collective-permute-start.2
  27.1 1.9 collective-permute-start.3
  29.0 0.3 reshape.207.link_next_ref.link_ref
  29.3 0.3 reshape.208.diag_ref
  29.6 0.3 fusion.6.stencil_ref
  29.8 0.7 collective-permute-done.2.before_y_ref
  30.5 4.4 collective-permute-done.3.after_y_ref
  35.0 3.4 copy-done.1
  38.3 59.7 %galerkin_tiles.1 = bf16[256,128,128]{2,1,0:T(8,128)(2,1)S(1)} custom-call(s32[128]{0:T(128)S(1)} %multiply_add_fusion.1.slot_ref, bf16[32,1024,128]{2,1,0:T(8,128)(2,1)S(1)} %bitcast.127, f32[32,1,1024]{2,1,0:T(1,128)S(1)} %reshape.207.link_next_ref.link_ref, f32[32,1,1024]{2,1,0:T(1,128)S(1)} %reshape.207.link_next_ref.link_ref, ...), custom_call_target="tpu_custom_call" | custom-call | tf_op jit(solution)/shard_map/galerkin_tiles/pallas_call | solution.py:100
  98.0 0.0 copy-start
  98.0 3.4 copy-done
  101.5 0.9 copy.57
  102.4 10.4 %all-to-all-start.1 = ((bf16[128,2,4,128]{3,2,1,0:T(4,128)(2,1)}), bf16[128,2,4,128]{3,2,1,0:T(4,128)(2,1)S(1)}, u32[]{:S(2)}, u32[]{:S(2)}) async-start(bf16[128,2,4,128]{3,2,1,0:T(4,128)(2,1)} %copy.57), calls=%async_computation.1 | async-start | bytes 524288 | tf_op jit(solution)/shard_map/all_to_all | solution.py:325
  112.8 0.1 copy.52
  112.9 0.1 eq.129
  113.0 9.5 %all-to-all-done.1 = bf16[128,2,4,128]{3,2,1,0:T(4,128)(2,1)S(1)} async-done(((bf16[128,2,4,128]{3,2,1,0:T(4,128)(2,1)}), bf16[128,2,4,128]{3,2,1,0:T(4,128)(2,1)S(1)}, u32[]{:S(2)}, u32[]{:S(2)}) %all-to-all-start.1) | async-done | bytes 262176 | tf_op jit(solution)/shard_map/all_to_all | solution.py:325
  122.6 0.1 fusion.7
  122.7 0.1 copy.62
  122.8 0.2 convolution_bitcast_fusion
  123.0 0.2 copy.63
  123.2 0.2 reshape.225
  123.4 13.4 %all_to_all.20 = f32[32,4,512]{2,1,0:T(4,128)S(1)} all-to-all(f32[32,4,512]{2,1,0:T(4,128)S(1)} %reshape.225), channel_id=1, replica_groups=mesh['grp'=4,'sub'=32] {'sub'}, dimensions={0} | all-to-all | bytes 524288 | tf_op jit(solution)/shard_map/all_to_all | solution.py:335
  136.8 4.7 all-to-all-start
  141.4 0.0 all-reduce.2.cloned.1.call-start
  141.5 1.9 slice_select_fusion
  143.4 0.0 all-reduce.2.cloned.1.call-update
  143.4 0.0 all-gather.2.cloned.1.call-start
  143.5 171.4 %all-reduce.2.cloned.1.call-done = bf16[512,512]{1,0:T(8,128)(2,1)} async-done(((bf16[512,512]{1,0:T(8,128)(2,1)}), bf16[512,512]{1,0:T(8,128)(2,1)}) %all-reduce.2.cloned.1.call-update) | async-done | bytes 524304 | tf_op jit(solution)/shard_map/psum | solution.py:280
  314.9 1.3 copy.49
  316.2 1.4 abs_reduce_fusion
  317.5 1.3 select_add_fusion
  318.9 0.3 copy.51.pivot_ref
  319.2 59.4 %pivot_factor.1 = (f32[512,512]{1,0:T(8,128)S(1)}, f32[512,512]{1,0:T(8,128)S(1)}) custom-call(f32[512,512]{1,0:T(8,128)S(1)} %copy.51.pivot_ref), custom_call_target="tpu_custom_call" | custom-call | flops 10000000000 | bytes 3145728 | tf_op jit(solution)/shard_map/pivot_factor/pallas_call | solution.py:182
  378.6 0.1 reshape.215
  378.7 0.0 all-to-all-done
  378.7 2.7 fusion
  381.4 0.0 all-gather.2.cloned.1.call-update
  381.4 8.3 %all-to-all-start.3 = ((bf16[128,2,128,128]{3,2,1,0:T(8,128)(2,1)}), bf16[128,2,128,128]{3,2,1,0:T(8,128)(2,1)}, u32[]{:S(2)}, u32[]{:S(2)}) async-start(bf16[128,2,128,128]{3,2,1,0:T(8,128)(2,1)} %bitcast.126), calls=%async_computation.3 | async-start | bytes 16777216 | tf_op jit(solution)/shard_map/all_to_all | solution.py:327
  389.7 121.0 %all-gather.2.cloned.1.call-done.row_ref = bf16[4096,512]{1,0:T(8,128)(2,1)} async-done(((bf16[128,512]{1,0:T(8,128)(2,1)}), bf16[4096,512]{1,0:T(8,128)(2,1)}) %all-gather.2.cloned.1.call-update) | async-done | bytes 4194320 | tf_op jit(solution)/shard_map/all_gather | solution.py:346
  510.7 1.1 dynamic-slice_select_fusion
  511.9 0.7 collective-permute-start.6
  512.6 0.7 collective-permute-start.5
  513.3 1.3 collective-permute-start.4
  514.6 0.1 copy.48
  514.7 0.1 reshape.204.place_ref
  514.9 0.0 collective-permute-done.6
  514.9 0.0 collective-permute-done.5
  514.9 26.0 %collective-permute-done.4 = bf16[512,512]{1,0:T(8,128)(2,1)S(1)} collective-permute-done((bf16[512,512]{1,0:T(8,128)(2,1)S(1)}, bf16[512,512]{1,0:T(8,128)(2,1)S(1)}, u32[]{:S(2)}, u32[]{:S(2)}) %collective-permute-start.4) | collective-permute-done | bytes 524320 | tf_op jit(solution)/shard_map/ppermute | solution.py:358
  540.9 1.3 add_add_fusion.col_ref
  542.2 2.2 copy-done.2
  544.4 17.1 %trailing_front.1 = f32[4096,512]{1,0:T(8,128)} custom-call(s32[256]{0:T(256)S(1)} %reshape.204.place_ref, bf16[4096,512]{1,0:T(8,128)(2,1)S(1)} %copy-done.2, bf16[512,512]{1,0:T(8,128)(2,1)S(1)} %add_add_fusion.col_ref, bf16[4096,512]{1,0:T(8,128)(2,1)} %base_ref.1, bf16[256,128,128]{2,1,0:T(8,128)(2,1)} %bitcast.32.received_ref), custom_call_target="tpu_custom_call" | custom-call | tf_op jit(solution)/shard_map/trailing_front/pallas_call | solution.py:237
  (23 shorter events, 0.2 us)
Async XLA Ops:
  7.2 21.9 %copy-start.3 = (f32[32,32,32]{2,1,0:T(8,128)S(1)}, f32[32,32,32]{2,1,0:T(8,128)}, u32[]{:S(2)}) copy-start(f32[32,32,32]{2,1,0:T(8,128)} %param.7) | copy-start | bytes 393220
  7.2 22.1 %copy-start.4 = (f32[32,32,32]{2,1,0:T(8,128)S(1)}, f32[32,32,32]{2,1,0:T(8,128)}, u32[]{:S(2)}) copy-start(f32[32,32,32]{2,1,0:T(8,128)} %param.6) | copy-start | bytes 393220
  10.8 9.1 %collective-permute-start.1 = (bf16[32,32,128]{2,1,0:T(8,128)(2,1)S(1)}, bf16[32,32,128]{2,1,0:T(8,128)(2,1)S(1)}, u32[]{:S(2)}, u32[]{:S(2)}) collective-permute-start(bf16[32,32,128]{2,1,0:T(8,128)(2,1)S(1)} %get-tuple-element.26), channel_id=1, source_target_pairs={{32,0},{64,32},{96,64},{33,1},{65,33},{97,65},{34,2},{66,34},{98,6... | collective-permute-start | bytes 786440 | tf_op jit(solution)/shard_map/ppermute | solution.py:261
  12.8 8.7 %collective-permute-start = (bf16[32,32,128]{2,1,0:T(8,128)(2,1)S(1)}, bf16[32,32,128]{2,1,0:T(8,128)(2,1)S(1)}, u32[]{:S(2)}, u32[]{:S(2)}) collective-permute-start(bf16[32,32,128]{2,1,0:T(8,128)(2,1)S(1)} %get-tuple-element.25), channel_id=1, source_target_pairs={{0,32},{32,64},{64,96},{1,33},{33,65},{65,97},{2,34},{34,66},{66,9... | collective-permute-start | bytes 786440 | tf_op jit(solution)/shard_map/ppermute | solution.py:261
  21.5 9.0 %collective-permute-start.2 = (bf16[34,32,128]{2,1,0:T(8,128)(2,1)S(1)}, bf16[34,32,128]{2,1,0:T(8,128)(2,1)S(1)}, u32[]{:S(2)}, u32[]{:S(2)}) collective-permute-start(bf16[34,32,128]{2,1,0:T(8,128)(2,1)S(1)} %pad_maximum_fusion), channel_id=1, source_target_pairs={{0,1},{1,2},{2,3},{3,4},{4,5},{5,6},{6,7},{7,8},{8,9},{9,10},{10,1... | collective-permute-start | bytes 835592 | tf_op jit(solution)/shard_map/ppermute | solution.py:261
  27.1 7.9 %collective-permute-start.3 = (bf16[34,32,128]{2,1,0:T(8,128)(2,1)S(1)}, bf16[34,32,128]{2,1,0:T(8,128)(2,1)S(1)}, u32[]{:S(2)}, u32[]{:S(2)}) collective-permute-start(bf16[34,32,128]{2,1,0:T(8,128)(2,1)S(1)} %pad_maximum_fusion.1), channel_id=1, source_target_pairs={{1,0},{2,1},{3,2},{4,3},{5,4},{6,5},{7,6},{8,7},{9,8},{10,9},{11,1... | collective-permute-start | bytes 835592 | tf_op jit(solution)/shard_map/ppermute | solution.py:261
  34.9 3.4 copy-start.1
  98.0 3.4 copy-start
  102.4 20.2 %all-to-all-start.1 = ((bf16[128,2,4,128]{3,2,1,0:T(4,128)(2,1)}), bf16[128,2,4,128]{3,2,1,0:T(4,128)(2,1)S(1)}, u32[]{:S(2)}, u32[]{:S(2)}) async-start(bf16[128,2,4,128]{3,2,1,0:T(4,128)(2,1)} %copy.57), calls=%async_computation.1 | async-start | bytes 524288 | tf_op jit(solution)/shard_map/all_to_all | solution.py:325
  136.8 241.9 %all-to-all-start = ((bf16[32,128,512]{2,1,0:T(8,128)(2,1)}), bf16[32,128,512]{2,1,0:T(8,128)(2,1)}, u32[]{:S(2)}, u32[]{:S(2)}) async-start(bf16[32,128,512]{2,1,0:T(8,128)(2,1)} %bitcast.130), calls=%async_computation | async-start | bytes 8388608 | tf_op jit(solution)/shard_map/all_to_all | solution.py:281
  141.4 173.5 %all-reduce.2.cloned.1.call-start = ((), (), s32[]{:S(2)}) async-start(), calls=%async_computation.4 | async-start | bytes 1048576 | tf_op jit(solution)/shard_map/psum | solution.py:280
  143.4 367.4 %all-gather.2.cloned.1.call-start = ((), (), s32[]{:S(2)}) async-start(), calls=%async_computation.5 | async-start | bytes 4325376 | tf_op jit(solution)/shard_map/all_gather | solution.py:346
  381.4 160.8 %all-to-all-start.3 = ((bf16[128,2,128,128]{3,2,1,0:T(8,128)(2,1)}), bf16[128,2,128,128]{3,2,1,0:T(8,128)(2,1)}, u32[]{:S(2)}, u32[]{:S(2)}) async-start(bf16[128,2,128,128]{3,2,1,0:T(8,128)(2,1)} %bitcast.126), calls=%async_computation.3 | async-start | bytes 16777216 | tf_op jit(solution)/shard_map/all_to_all | solution.py:327
  511.9 3.0 collective-permute-start.6
  512.6 2.3 collective-permute-start.5
  513.3 27.6 %collective-permute-start.4 = (bf16[512,512]{1,0:T(8,128)(2,1)S(1)}, bf16[512,512]{1,0:T(8,128)(2,1)S(1)}, u32[]{:S(2)}, u32[]{:S(2)}) collective-permute-start(bf16[512,512]{1,0:T(8,128)(2,1)S(1)} %dynamic-slice_select_fusion), channel_id=1, source_target_pairs={{0,32},{1,33},{2,34},{3,35},{4,36},{5,37},{6,38},{7,39},{40,72},{4... | collective-permute-start | bytes 1572872 | tf_op jit(solution)/shard_map/ppermute | solution.py:358
  542.2 2.2 copy-start.2
Sparse Core Ops, SparseCore 0:
  147.0 167.8 all-reduce.1
  381.5 129.1 all-gather.1

commit v2 on v1

--- a/solution.py
+++ b/solution.py
@@ -256,9 +256,339 @@
     )(place, panel_rows, panel_cols, base, received)
 
 
-def shifted(x, axis, count, up):
-    pairs = [(i, i + 1) if up else (i + 1, i) for i in range(count - 1)]
-    return lax.ppermute(x, axis, pairs)
+def at(group, member):
+    return {"grp": group, "sub": member}
+
+
+def opening_kernel(
+    high_x, low_x, high_y, low_y, base_ref,
+    before_x, after_x, before_y, after_y, lead_ref, rows_ref,
+    halo_send, halo_recv, lead_send, lead_recv, base_send, base_recv, own_sem,
+):
+    groups, members = 4, 32
+    group = lax.axis_index("grp")
+    member = lax.axis_index("sub")
+    barrier = pltpu.get_barrier_semaphore()
+    sides = [(dg, ds) for dg in (-1, 0, 1) for ds in (-1, 0, 1) if (dg, ds) != (0, 0)]
+
+    def exists(dg, ds):
+        g, s = group + dg, member + ds
+        return (g >= 0) & (g < groups) & (s >= 0) & (s < members)
+
+    def greet(d, carry):
+        pl.semaphore_signal(barrier, 1, device_id=at(group, lax.rem(member + d, members)))
+        return carry
+
+    lax.fori_loop(1, members, greet, 0)
+    for d in range(1, groups):
+        pl.semaphore_signal(barrier, 1, device_id=at(lax.rem(group + d, groups), member))
+    for dg, ds in sides:
+        if dg and ds:
+            @pl.when(exists(dg, ds))
+            def _():
+                pl.semaphore_signal(barrier, 1, device_id=at(group + dg, member + ds))
+
+    near_groups = 2 - jnp.where(group == 0, 1, 0) - jnp.where(group == groups - 1, 1, 0)
+    near_members = 2 - jnp.where(member == 0, 1, 0) - jnp.where(member == members - 1, 1, 0)
+    pl.semaphore_wait(barrier, members - 1 + groups - 1 + near_groups * near_members)
+
+    def piece(m):
+        return pl.ds(pl.multiple_of(16 * m, 16), 16)
+
+    def lead_copy(source, m, k, g, s):
+        return pltpu.make_async_remote_copy(
+            source.at[piece(m)], lead_ref.at[piece(m)], lead_send.at[k], lead_recv.at[m],
+            device_id=at(g, s),
+        )
+
+    def base_copy(m):
+        rows = pl.ds(pl.multiple_of(128 * m, 128), 128)
+        return pltpu.make_async_remote_copy(
+            base_ref.at[rows], rows_ref, base_send.at[m], base_recv, device_id=at(group, m)
+        )
+
+    own_lead = pltpu.make_async_copy(base_ref.at[pl.ds(0, 16)], lead_ref.at[pl.ds(0, 16)], own_sem.at[0])
+    own_rows = pltpu.make_async_copy(base_ref.at[pl.ds(0, 128)], rows_ref, own_sem.at[1])
+    root = (group == 0) & (member == 0)
+
+    @pl.when(root)
+    def _():
+        own_lead.start()
+
+        def send(m, carry):
+            lead_copy(base_ref, m, m, 0, m).start()
+            return carry
+
+        lax.fori_loop(1, members, send, 0)
+
+    def halo(dg, ds):
+        k = sides.index((dg, ds))
+        if ds == 0:
+            source, target = (high_x, before_x) if dg == 1 else (low_x, after_x)
+        else:
+            if dg == 0:
+                source = high_y if ds == 1 else low_y
+                place = pl.ds(32, 1024)
+            else:
+                face = high_x if dg == 1 else low_x
+                source = face.at[pl.ds(992 if ds == 1 else 0, 32)]
+                place = pl.ds(0 if dg == 1 else 1056, 32)
+            target = (before_y if ds == 1 else after_y).at[place]
+        return pltpu.make_async_remote_copy(
+            source, target, halo_send.at[k], halo_recv.at[k], device_id=at(group + dg, member + ds)
+        )
+
+    for dg, ds in sides:
+        @pl.when(exists(dg, ds))
+        def _():
+            halo(dg, ds).start()
+
+        @pl.when(jnp.logical_not(exists(-dg, -ds)))
+        def _():
+            if ds == 0:
+                target = before_x if dg == 1 else after_x
+                target[...] = jnp.zeros_like(target)
+            else:
+                target = before_y if ds == 1 else after_y
+                place = pl.ds(32, 1024) if dg == 0 else pl.ds(0 if dg == 1 else 1056, 32)
+                target[place, :] = jnp.zeros((1024 if dg == 0 else 32, 128), BF)
+
+    @pl.when(member == 0)
+    def _():
+        own_rows.start()
+
+        def send(m, carry):
+            base_copy(m).start()
+            return carry
+
+        lax.fori_loop(1, members, send, 0)
+
+    @pl.when(root)
+    def _():
+        own_lead.wait()
+
+    @pl.when(jnp.logical_not(root))
+    def _():
+        lead_copy(lead_ref, member, 0, group, member).wait_recv()
+
+    @pl.when(group == 0)
+    def _():
+        for g in range(1, groups):
+            lead_copy(lead_ref, member, 64 + g, g, member).start()
+
+    def spread(d, carry):
+        lead_copy(lead_ref, member, 32 + d, group, lax.rem(member + d, members)).start()
+        return carry
+
+    lax.fori_loop(1, members, spread, 0)
+
+    for dg, ds in sides:
+        @pl.when(exists(-dg, -ds))
+        def _():
+            halo(dg, ds).wait_recv()
+
+        @pl.when(exists(dg, ds))
+        def _():
+            halo(dg, ds).wait_send()
+
+    def gather(d, carry):
+        lead_copy(lead_ref, lax.rem(member + d, members), 0, group, member).wait_recv()
+        lead_copy(lead_ref, member, 32 + d, group, member).wait_send()
+        return carry
+
+    lax.fori_loop(1, members, gather, 0)
+
+    @pl.when(group == 0)
+    def _():
+        for g in range(1, groups):
+            lead_copy(lead_ref, member, 64 + g, g, member).wait_send()
+
+    @pl.when(root)
+    def _():
+        def sent(m, carry):
+            lead_copy(base_ref, m, m, 0, m).wait_send()
+            return carry
+
+        lax.fori_loop(1, members, sent, 0)
+
+    @pl.when(member == 0)
+    def _():
+        def sent(m, carry):
+            base_copy(m).wait_send()
+            return carry
+
+        lax.fori_loop(1, members, sent, 0)
+        own_rows.wait()
+
+    @pl.when(member > 0)
+    def _():
+        base_copy(member).wait_recv()
+
+
+def opening(high_x, low_x, high_y, low_y, base_front):
+    vmem = pl.BlockSpec(memory_space=pltpu.VMEM)
+    dma = pltpu.SemaphoreType.DMA
+    return pl.pallas_call(
+        opening_kernel,
+        out_shape=[
+            jax.ShapeDtypeStruct((1024, 128), BF),
+            jax.ShapeDtypeStruct((1024, 128), BF),
+            jax.ShapeDtypeStruct((1088, 128), BF),
+            jax.ShapeDtypeStruct((1088, 128), BF),
+            jax.ShapeDtypeStruct((512, 512), BF),
+            jax.ShapeDtypeStruct((128, 512), BF),
+        ],
+        in_specs=[vmem] * 4 + [pl.BlockSpec(memory_space=pl.ANY)],
+        out_specs=[vmem] * 6,
+        scratch_shapes=[
+            dma((8,)), dma((8,)), dma((68,)), dma((32,)), dma((32,)), dma, dma((2,)),
+        ],
+        compiler_params=pltpu.CompilerParams(
+            collective_id=0, has_side_effects=True, vmem_limit_bytes=16 * 2**20
+        ),
+        name="opening",
+    )(high_x, low_x, high_y, low_y, base_front)
+
+
+def panel_kernel(
+    panel_ref, rows_ref, cols_ref, send, recv, fold_send, fold_recv, col_send, col_recv, own_sem
+):
+    groups, members, chips = 4, 32, 16
+    group = lax.axis_index("grp")
+    member = lax.axis_index("sub")
+    chip = member // 2
+    core = lax.rem(member, 2)
+    live = member // 8 <= group
+    source_group = member // 8
+    barrier = pltpu.get_barrier_semaphore()
+
+    def greet(d, carry):
+        pl.semaphore_signal(barrier, 1, device_id=at(group, lax.rem(member + d, members)))
+        return carry
+
+    lax.fori_loop(1, members, greet, 0)
+
+    @pl.when(source_group < group)
+    def _():
+        for i in range(4):
+            pl.semaphore_signal(
+                barrier, 1, device_id=at(source_group, lax.rem(member, 8) * 4 + i)
+            )
+
+    pl.semaphore_wait(barrier, members - 1 + groups - 1 - group)
+
+    def block(m):
+        return pl.ds(pl.multiple_of(128 * m, 128), 128)
+
+    def row_copy(m, k, s):
+        return pltpu.make_async_remote_copy(
+            panel_ref, rows_ref.at[block(m)], send.at[k], recv.at[m // 2], device_id=at(group, s)
+        )
+
+    def fold_copy(m, source):
+        return pltpu.make_async_remote_copy(
+            source, rows_ref.at[block(m)], fold_send.at[m // 2], fold_recv.at[m // 2],
+            device_id=at(group, chip * 2 + 1 - core),
+        )
+
+    def other(d):
+        return lax.rem(chip + d, chips) * 2 + core
+
+    target = group * 8 + member // 4
+    quarter = lax.rem(member, 4)
+
+    def col_copy(g, q, s):
+        return pltpu.make_async_remote_copy(
+            panel_ref, cols_ref.at[block(q)], col_send.at[g], col_recv.at[q], device_id=at(g, s)
+        )
+
+    def spread(d, carry):
+        @pl.when(other(d) // 8 <= group)
+        def _():
+            row_copy(member, d, other(d)).start()
+
+        return carry
+
+    lax.fori_loop(1, chips, spread, 0)
+
+    for g in range(groups):
+        @pl.when((g >= group) & jnp.logical_not((g == group) & (target == member)))
+        def _():
+            col_copy(g, quarter, target).start()
+
+    own_cols = pltpu.make_async_copy(panel_ref, cols_ref.at[block(quarter)], own_sem.at[0])
+    own_rows = pltpu.make_async_copy(panel_ref, rows_ref.at[block(member)], own_sem.at[1])
+
+    @pl.when(target == member)
+    def _():
+        own_cols.start()
+
+    own_rows.start()
+
+    @pl.when(live)
+    def _():
+        fold_copy(member, panel_ref).start()
+
+        def fold(d, carry):
+            m = other(d)
+            row_copy(m, 0, member).wait_recv()
+            fold_copy(m, rows_ref.at[block(m)]).start()
+            return carry
+
+        lax.fori_loop(1, chips, fold, 0)
+
+        def folded(d, carry):
+            m = lax.rem(chip + d, chips) * 2
+            fold_copy(m + 1 - core, panel_ref).wait_recv()
+            fold_copy(m + core, panel_ref).wait_send()
+            return carry
+
+        lax.fori_loop(0, chips, folded, 0)
+
+    def sent(d, carry):
+        @pl.when(other(d) // 8 <= group)
+        def _():
+            row_copy(member, d, other(d)).wait_send()
+
+        return carry
+
+    lax.fori_loop(1, chips, sent, 0)
+    for g in range(groups):
+        @pl.when((g >= group) & jnp.logical_not((g == group) & (target == member)))
+        def _():
+            col_copy(g, quarter, target).wait_send()
+
+    for i in range(4):
+        source = lax.rem(member, 8) * 4 + i
+        itself = (source_group == group) & (source == member)
+
+        @pl.when((source_group <= group) & jnp.logical_not(itself))
+        def _():
+            col_copy(group, i, member).wait_recv()
+
+    @pl.when(target == member)
+    def _():
+        own_cols.wait()
+
+    own_rows.wait()
+
+
+def panel_spread(panel):
+    dma = pltpu.SemaphoreType.DMA
+    anywhere = pl.BlockSpec(memory_space=pl.ANY)
+    return pl.pallas_call(
+        panel_kernel,
+        out_shape=[jax.ShapeDtypeStruct((4096, 512), BF), jax.ShapeDtypeStruct((512, 512), BF)],
+        in_specs=[pl.BlockSpec(memory_space=pltpu.VMEM)],
+        out_specs=[anywhere, anywhere],
+        scratch_shapes=[
+            dma((16,)), dma((16,)), dma((16,)), dma((16,)), dma((4,)), dma((4,)), dma((2,)),
+        ],
+        compiler_params=pltpu.CompilerParams(
+            collective_id=1, has_side_effects=True, vmem_limit_bytes=16 * 2**20
+        ),
+        name="panel_spread",
+    )(panel)
 
 
 def arrivals(owner_ids, local_block, owner):
@@ -276,23 +606,16 @@
     member = lax.axis_index("sub")
     me = group * members + member
 
-    lead = jnp.where(me == 0, base_front[:512], jnp.zeros((512, 512), BF))
-    lead = lax.psum(lead, ("grp", "sub"))
-    base_rows = lax.all_to_all(
-        base_front.reshape(members, 128, 512), "sub", split_axis=0, concat_axis=0, tiled=True
-    )[0]
-
     def scaled(b, w):
-        return (w[..., None] * b.astype(F32)).astype(BF)
-
-    before_x = shifted(scaled(basis_cols[31], link_weight[31]), "grp", groups, True)
-    after_x = shifted(scaled(basis_cols[0], link_weight[0]), "grp", groups, False)
-    high_y = scaled(basis_cols[:, 31], link_weight[:, 31])
-    low_y = scaled(basis_cols[:, 0], link_weight[:, 0])
-    high_y = jnp.concatenate([before_x[None, 31], high_y, after_x[None, 31]], axis=0)
-    low_y = jnp.concatenate([before_x[None, 0], low_y, after_x[None, 0]], axis=0)
-    before_y = shifted(high_y, "sub", members, True)
-    after_y = shifted(low_y, "sub", members, False)
+        return (w[..., None] * b.astype(F32)).astype(BF).reshape(1024, 128)
+
+    before_x, after_x, before_y, after_y, lead, base_rows = opening(
+        scaled(basis_cols[31], link_weight[31]),
+        scaled(basis_cols[0], link_weight[0]),
+        scaled(basis_cols[:, 31], link_weight[:, 31]),
+        scaled(basis_cols[:, 0], link_weight[:, 0]),
+        base_front,
+    )
 
     listed = block_lists.reshape(devices, 128, 2)
     row_block = listed[:, :, 0]
@@ -313,17 +636,17 @@
         basis_cols.reshape(32, 1024, 128),
         link_weight.reshape(32, 1, 1024),
         diag_weight.reshape(32, 1, 1024),
-        before_y,
-        after_y,
-        before_x.reshape(1024, 128),
-        after_x.reshape(1024, 128),
+        before_y.reshape(34, 32, 128),
+        after_y.reshape(34, 32, 128),
+        before_x,
+        after_x,
     )
 
+    outgoing, lead = lax.optimization_barrier((outgoing, lead))
     strips = outgoing.reshape(groups, members, 2, 128, 128)[:, 0]
     strips = strips.reshape(groups, 2, members, 4, 128).transpose(0, 2, 1, 3, 4)
     strips = strips.reshape(devices, 2, 4, 128)
     strips = lax.all_to_all(strips, ("grp", "sub"), split_axis=0, concat_axis=0, tiled=True)
-    strips, outgoing = lax.optimization_barrier((strips, outgoing))
     received = lax.all_to_all(
         outgoing.reshape(devices, 2, 128, 128), ("grp", "sub"), split_axis=0, concat_axis=0, tiled=True
     ).reshape(256, 128, 128)
@@ -343,20 +666,8 @@
     in_lead = (group == 0) & (member < 4)
     own_factor = lax.dynamic_slice_in_dim(factor, 128 * jnp.minimum(member, 3), 128, 0)
     panel = jnp.where(in_lead, own_factor, solved).astype(BF)
-    panel_rows = lax.all_gather(panel, "sub", axis=0, tiled=True)
-
-    source = member // 8
-    piece = lax.dynamic_slice_in_dim(panel_rows, member % 8 * 512, 512, 0)
-    panel_cols = jnp.where(group == source, piece, jnp.zeros_like(piece))
-    total = panel_cols
-    for ahead in range(1, groups):
-        pairs = [
-            (s // 8 * members + s, (s // 8 + ahead) * members + s)
-            for s in range(members)
-            if s // 8 + ahead < groups
-        ]
-        total = total + lax.ppermute(panel_cols, ("grp", "sub"), pairs)
-    trailing = trailing_front(place, panel_rows, total, base_front, received)
+    panel_rows, panel_cols = panel_spread(panel)
+    trailing = trailing_front(place, panel_rows, panel_cols, base_front, received)
     return (trailing, panel)
 
 

time: 569 us -> 328 us (0.58)
  the two profiles are of different devices: /device:TPU:9 before, /device:TPU:121 now
where the time goes in v2:
time: 328 us; the launch traced here: 327 us
  Pallas kernels  246 us (75%)
  starting transfers between devices  33.1 us (10%)
  local copies, waits for them, and re-layouts  23.6 us (7%)
  blocking collectives  13.4 us (4%)
  waiting for transfers between devices  6.27 us (2%)
    pallas_call x1, Pallas kernels, panel_spread(): pl.pallas_call(panel_kernel, out_shape=[jax.ShapeDtypeStruct((4096, 512),...  85 us
    pallas_call x1, Pallas kernels, galerkin_tiles(): pl.pallas_call(tile_kernel, out_shape=jax.ShapeDtypeStruct((256, 128, 128...  59.7 us
    pallas_call x1, Pallas kernels, pivot_factor(): pl.pallas_call(factor_kernel, out_shape=[jax.ShapeDtypeStruct((size, size...  59.4 us
    pallas_call x1, Pallas kernels, opening(): pl.pallas_call(opening_kernel, out_shape=[jax.ShapeDtypeStruct((1024, 128...  24.9 us
    all_to_all x1, starting transfers between devices, per_device(): lax.all_to_all(strips, ('grp', 'sub'), split_axis=0, concat_axis=0, tiled...  24 us
    pallas_call x1, Pallas kernels, trailing_front(): pl.pallas_call(final_kernel, out_shape=jax.ShapeDtypeStruct((4096, 512),...  17.1 us
    unnamed x15, local copies, waits for them, and re-layouts  14 us
    all_to_all x1, blocking collectives, per_device(): lax.all_to_all(strips, 'sub', split_axis=0, concat_axis=0, tiled=True)  13.4 us
  transfers between devices with their start and end apart: 2, of which 1 were waited for; matrix products, arithmetic and copies ran while one was open for 1% of the time, Pallas kernels for 44%

profile of v2, /device:TPU:121, one launch (start us, length us, event | category | flops | bytes accessed | tf_op | source)
XLA Modules:
  0.0 327.1 jit_solution(9875063714929095194)
XLA Ops:
  0.7 1.1 slice_reduce_fusion
  1.7 0.7 fusion.45
  2.5 1.3 reshape.217.link_next_ref.link_ref
  3.8 1.1 fusion.43
  4.9 1.1 fusion.44
  5.9 0.1 mul.76
  6.0 0.1 mul.73
  6.1 0.1 mul.70
  6.2 0.1 mul.67
  6.2 1.3 reshape.218.diag_ref
  7.5 0.9 copy.67
  8.4 0.2 select_reduce_fusion.5
  8.6 0.2 convert_reduce_fusion
  8.8 0.3 fusion.6.stencil_ref
  9.1 0.3 fusion.1
  9.5 0.3 fusion.3
  9.8 0.0 copy-start.1
  9.8 2.2 copy-done.1
  12.0 24.9 %opening.1 = (bf16[1024,128]{1,0:T(8,128)(2,1)S(1)}, bf16[1024,128]{1,0:T(8,128)(2,1)S(1)}, bf16[1088,128]{1,0:T(8,128)(2,1)S(1)}, bf16[1088,128]{1,0:T(8,128)(2...) custom-call(bf16[1024,128]{1,0:T(8,128)(2,1)S(1)} %get-tuple-element.50.high_x, ...), custom_call_target="tpu_custom_call" | custom-call | tf_op jit(solution)/shard_map/opening/pallas_call | solution.py:431
  36.9 0.0 copy-start.2
  36.9 3.4 %copy-done.2 = bf16[32,32,32,128]{3,2,1,0:T(8,128)(2,1)S(1)} copy-done((bf16[32,32,32,128]{3,2,1,0:T(8,128)(2,1)S(1)}, bf16[32,32,32,128]{3,2,1,0:T(8,128)(2,1)}, u32[]{:S(2)}) %copy-start.2) | copy-done | bytes 8388632
  40.3 59.7 %galerkin_tiles.1 = bf16[256,128,128]{2,1,0:T(8,128)(2,1)S(1)} custom-call(s32[128]{0:T(128)S(1)} %multiply_add_fusion.1.slot_ref, bf16[32,1024,128]{2,1,0:T(8,128)(2,1)S(1)} %bitcast.107, f32[32,1,1024]{2,1,0:T(1,128)S(1)} %reshape.217.link_next_ref.link_ref, f32[32,1,1024]{2,1,0:T(1,128)S(1)} %reshape.217.link_next_ref.link_ref, ...), custom_call_target="tpu_custom_call" | custom-call | tf_op jit(solution)/shard_map/galerkin_tiles/pallas_call | solution.py:100
  100.0 0.0 copy-start
  100.0 3.4 %copy-done = bf16[256,128,128]{2,1,0:T(8,128)(2,1)} copy-done((bf16[256,128,128]{2,1,0:T(8,128)(2,1)}, bf16[256,128,128]{2,1,0:T(8,128)(2,1)S(1)}, u32[]{:S(2)}) %copy-start) | copy-done | bytes 8388632
  103.4 0.9 copy.53
  104.3 24.0 %all-to-all-start = ((bf16[128,2,4,128]{3,2,1,0:T(4,128)(2,1)}), bf16[128,2,4,128]{3,2,1,0:T(4,128)(2,1)S(1)}, u32[]{:S(2)}, u32[]{:S(2)}) async-start(bf16[128,2,4,128]{3,2,1,0:T(4,128)(2,1)} %copy.53), calls=%async_computation | async-start | bytes 524288 | tf_op jit(solution)/shard_map/all_to_all | solution.py:649
  128.4 0.1 select_reduce_fusion.2
  128.5 0.2 select_reduce_fusion.1
  128.7 0.1 copy.50
  128.9 0.1 eq.125
  129.0 6.3 %all-to-all-done = bf16[128,2,4,128]{3,2,1,0:T(4,128)(2,1)S(1)} async-done(((bf16[128,2,4,128]{3,2,1,0:T(4,128)(2,1)}), bf16[128,2,4,128]{3,2,1,0:T(4,128)(2,1)S(1)}, u32[]{:S(2)}, u32[]{:S(2)}) %all-to-all-start) | async-done | bytes 262176 | tf_op jit(solution)/shard_map/all_to_all | solution.py:649
  135.3 0.1 fusion.7
  135.4 0.1 copy.58
  135.5 0.2 convolution_bitcast_fusion
  135.8 0.2 copy.59
  135.9 0.2 reshape.234
  136.1 13.4 %all_to_all.15 = f32[32,4,512]{2,1,0:T(4,128)} all-to-all(f32[32,4,512]{2,1,0:T(4,128)S(1)} %reshape.234), channel_id=1, replica_groups=mesh['grp'=4,'sub'=32] {'sub'}, dimensions={0} | all-to-all | bytes 524288 | tf_op jit(solution)/shard_map/all_to_all | solution.py:658
  149.5 9.1 %all-to-all-start.2 = ((bf16[128,2,128,128]{3,2,1,0:T(8,128)(2,1)}), bf16[128,2,128,128]{3,2,1,0:T(8,128)(2,1)}, u32[]{:S(2)}, u32[]{:S(2)}) async-start(bf16[128,2,128,128]{3,2,1,0:T(8,128)(2,1)} %bitcast.106), calls=%async_computation.2 | async-start | bytes 16777216 | tf_op jit(solution)/shard_map/all_to_all | solution.py:650
  158.6 0.1 copy.45
  158.7 0.1 reshape.215.place_ref
  158.9 0.2 copy.46
  159.1 0.2 copy.48
  159.3 0.3 abs_reduce_fusion
  159.6 0.3 copy.49
  160.0 0.1 select_add_fusion.pivot_ref
  160.2 0.0 copy-start.6
  160.2 59.4 %pivot_factor.1 = (f32[512,512]{1,0:T(8,128)S(1)}, f32[512,512]{1,0:T(8,128)S(1)}) custom-call(f32[512,512]{1,0:T(8,128)S(1)} %select_add_fusion.pivot_ref), custom_call_target="tpu_custom_call" | custom-call | flops 10000000000 | bytes 3145728 | tf_op jit(solution)/shard_map/pivot_factor/pallas_call | solution.py:182
  219.5 0.0 copy-done.6
  219.6 0.1 reshape.225
  219.7 1.1 fusion.panel_ref
  220.8 0.0 copy-start.5
  220.8 85.0 %panel_spread.1 = (bf16[4096,512]{1,0:T(8,128)(2,1)S(1)}, bf16[512,512]{1,0:T(8,128)(2,1)S(1)}) custom-call(bf16[128,512]{1,0:T(8,128)(2,1)S(1)} %fusion.panel_ref), custom_call_target="tpu_custom_call" | custom-call | tf_op jit(solution)/shard_map/panel_spread/pallas_call | solution.py:579
  305.8 0.0 copy-start.3
  305.8 2.0 copy-done.3
  307.8 0.0 all-to-all-done.2
  307.8 0.0 copy-start.4
  307.8 2.2 copy-done.4
  310.0 17.1 %trailing_front.1 = f32[4096,512]{1,0:T(8,128)} custom-call(s32[256]{0:T(256)S(1)} %reshape.215.place_ref, bf16[4096,512]{1,0:T(8,128)(2,1)S(1)} %copy-done.4, bf16[512,512]{1,0:T(8,128)(2,1)S(1)} %get-tuple-element.25.col_ref, bf16[4096,512]{1,0:T(8,128)(2,1)} %base_ref.3, bf16[256,128,128]{2,1,0:T(8,128)(2,1)} %bitcast.26.received_ref), custom_call_target="tpu_custom_call" | custom-call | tf_op jit(solution)/shard_map/trailing_front/pallas_call | solution.py:237
  327.1 0.0 copy-done.5
  (13 shorter events, 0.1 us)
Async XLA Ops:
  9.8 2.2 copy-start.1
  36.9 3.4 %copy-start.2 = (bf16[32,32,32,128]{3,2,1,0:T(8,128)(2,1)S(1)}, bf16[32,32,32,128]{3,2,1,0:T(8,128)(2,1)}, u32[]{:S(2)}) copy-start(bf16[32,32,32,128]{3,2,1,0:T(8,128)(2,1)} %param.5) | copy-start | bytes 25165828
  100.0 3.4 %copy-start = (bf16[256,128,128]{2,1,0:T(8,128)(2,1)}, bf16[256,128,128]{2,1,0:T(8,128)(2,1)S(1)}, u32[]{:S(2)}) copy-start(bf16[256,128,128]{2,1,0:T(8,128)(2,1)S(1)} %galerkin_tiles.1) | copy-start | bytes 25165828
  104.3 31.0 %all-to-all-start = ((bf16[128,2,4,128]{3,2,1,0:T(4,128)(2,1)}), bf16[128,2,4,128]{3,2,1,0:T(4,128)(2,1)S(1)}, u32[]{:S(2)}, u32[]{:S(2)}) async-start(bf16[128,2,4,128]{3,2,1,0:T(4,128)(2,1)} %copy.53), calls=%async_computation | async-start | bytes 524288 | tf_op jit(solution)/shard_map/all_to_all | solution.py:649
  149.5 158.2 %all-to-all-start.2 = ((bf16[128,2,128,128]{3,2,1,0:T(8,128)(2,1)}), bf16[128,2,128,128]{3,2,1,0:T(8,128)(2,1)}, u32[]{:S(2)}, u32[]{:S(2)}) async-start(bf16[128,2,128,128]{3,2,1,0:T(8,128)(2,1)} %bitcast.106), calls=%async_computation.2 | async-start | bytes 16777216 | tf_op jit(solution)/shard_map/all_to_all | solution.py:650
  160.2 59.4 %copy-start.6 = (f32[32,4,512]{2,1,0:T(4,128)S(1)}, f32[32,4,512]{2,1,0:T(4,128)}, u32[]{:S(2)}) copy-start(f32[32,4,512]{2,1,0:T(4,128)} %all_to_all.15) | copy-start | bytes 786436
  220.8 106.3 %copy-start.5 = (bf16[128,512]{1,0:T(8,128)(2,1)}, bf16[128,512]{1,0:T(8,128)(2,1)S(1)}, u32[]{:S(2)}) copy-start(bf16[128,512]{1,0:T(8,128)(2,1)S(1)} %fusion.panel_ref) | copy-start | bytes 393220
  305.8 2.0 copy-start.3
  307.8 2.2 copy-start.4

commit v3 on v2

--- a/solution.py
+++ b/solution.py
@@ -22,154 +22,177 @@
 
 
 def tile_kernel(
-    slot_ref, basis_ref, link_next_ref, link_ref, diag_ref, before_y_ref, after_y_ref,
-    before_x_ref, after_x_ref, stencil_ref, eye_ref, out_ref,
+    slot_ref, basis_ref, link_ref, diag_ref, before_y_ref, after_y_ref,
+    before_x_ref, after_x_ref, stencil_ref, out_ref,
     scaled_t, basis_t, partial, stage, sems,
 ):
     step = pl.program_id(0)
-    steps = pl.num_programs(0)
-    here = lax.rem(step, 2)
-    there = lax.rem(step + 1, 2)
-    eye = eye_ref[...]
     gap = jnp.zeros((96, 128), BF)
-    first = jnp.concatenate([gap, before_y_ref[0]], axis=0)
-    last = jnp.concatenate([after_y_ref[0], gap], axis=0)
-    scaled_t[here, :, 0:128] = dotb(eye, first, NT).astype(BF)
-    scaled_t[here, :, 1152:1280] = dotb(eye, last, NT).astype(BF)
-
-    @pl.when((step > 0) & (step < steps - 1))
-    def _():
-        turned = dotb(eye, basis_ref[0], NT)
-        basis_t[here] = turned.astype(BF)
-        scaled_t[here, :, 128:1152] = (turned * link_next_ref[0]).astype(BF)
-
-    @pl.when(step == 0)
-    def _():
-        scaled_t[here, :, 128:1152] = dotb(eye, before_x_ref[...], NT).astype(BF)
-
-    @pl.when(step == steps - 1)
-    def _():
-        scaled_t[here, :, 128:1152] = dotb(eye, after_x_ref[...], NT).astype(BF)
-
-    ring = lax.rem(step, 3)
-    for q in range(4):
-        partial[ring, :, 256 * q:256 * q + 256] = dotb(
-            scaled_t[here, :, 256 * q:256 * q + 512], stencil_ref[...], NN
-        )
-
-    def copy_out(buffer, q, slot):
-        return pltpu.make_async_copy(stage.at[buffer, q], out_ref.at[slot], sems.at[buffer, q])
-
-    @pl.when(step >= 2)
-    def _():
-        @pl.when(step >= 4)
-        def _():
-            for q in range(4):
-                copy_out(here, q, 0).wait()
-
+
+    def sides(slot, plane):
+        first = jnp.concatenate([gap, before_y_ref[plane + 1]], axis=0)
+        last = jnp.concatenate([after_y_ref[plane + 1], gap], axis=0)
+        scaled_t[slot, :, 0:128] = first.T
+        scaled_t[slot, :, 1152:1280] = last.T
+
+    def spread(slot, ring):
+        windows = [scaled_t[slot, :, 256 * q:256 * q + 512] for q in range(4)]
+        sums = dotb(jnp.concatenate(windows, axis=0), stencil_ref[...], NN)
+        for q in range(4):
+            partial[ring, :, 256 * q:256 * q + 256] = sums[128 * q:128 * q + 128]
+
+    def copy_out(slot, q, target):
+        return pltpu.make_async_copy(stage.at[slot, q], out_ref.at[target], sems.at[slot, q])
+
+    def wait(slot):
+        for q in range(4):
+            copy_out(slot, q, 0).wait()
+
+    def start(slot, plane):
+        for q in range(4):
+            copy_out(slot, q, slot_ref[plane * 4 + q]).start()
+
+    def finish(plane, slot, low, mid, high):
+        link = link_ref[plane]
+        diag = diag_ref[plane]
         for q in range(4):
             cells = slice(256 * q, 256 * q + 256)
-            around = partial[0, :, cells] + partial[1, :, cells] + partial[2, :, cells]
-            around = around - scaled_t[there, :, 128 + 256 * q:384 + 256 * q].astype(F32)
-            own = basis_t[there, :, cells]
-            image = diag_ref[0, :, cells] * own.astype(F32) - link_ref[0, :, cells] * around
-            high = image.astype(BF)
-            low = (image - high.astype(F32)).astype(BF)
-            stage[here, q] = (dotb(own, high, NT) + dotb(own, low, NT)).astype(BF)
-            copy_out(here, q, slot_ref[(step - 2) * 4 + q]).start()
-
-    @pl.when(step == steps - 1)
-    def _():
-        for q in range(4):
-            copy_out(there, q, 0).wait()
-            copy_out(here, q, 0).wait()
+            around = partial[low, :, cells] + partial[mid, :, cells] + partial[high, :, cells]
+            around = around - scaled_t[slot, :, 128 + 256 * q:384 + 256 * q].astype(F32)
+            own = basis_t[slot, :, cells]
+            image = diag[:, cells] * own.astype(F32) - link[:, cells] * around
+            head = image.astype(BF)
+            tail = (image - head.astype(F32)).astype(BF)
+            stage[slot, q] = (dotb(own, head, NT) + dotb(own, tail, NT)).astype(BF)
+
+    @pl.when(step == 0)
+    def _():
+        sides(1, -1)
+        scaled_t[1, :, 128:1152] = before_x_ref[...].T
+        spread(1, 3)
+
+    for u in range(4):
+        plane = step * 4 + u
+        slot = u % 2
+        turned = basis_ref[u].T
+        basis_t[slot] = turned
+        scaled_t[slot, :, 128:1152] = (turned.astype(F32) * link_ref[plane]).astype(BF)
+        sides(slot, plane)
+        spread(slot, u)
+        if u < 3:
+            pl.when(step > 0)(functools.partial(wait, 1 - slot))
+        else:
+            wait(1 - slot)
+        finish(jnp.maximum(plane - 1, 0), 1 - slot, (u + 2) % 4, (u + 3) % 4, u)
+        if u == 0:
+            pl.when(step > 0)(functools.partial(start, 1 - slot, plane - 1))
+        else:
+            start(1 - slot, plane - 1)
+
+    @pl.when(step == pl.num_programs(0) - 1)
+    def _():
+        sides(0, 32)
+        scaled_t[0, :, 128:1152] = after_x_ref[...].T
+        spread(0, 0)
+        wait(1)
+        finish(31, 1, 2, 3, 0)
+        start(1, 31)
+        wait(0)
+        wait(1)
 
 
 def galerkin_tiles(slots, basis, link, diag, before_y, after_y, before_x, after_x):
-    planes = basis.shape[0]
     k = jnp.arange(512)[:, None]
     n = jnp.arange(256)[None, :]
     stencil = (
         (jnp.abs(k // 32 - 4 - n // 32) <= 1) & (jnp.abs(k % 32 - n % 32) <= 1)
     ).astype(BF)
-    eye = jnp.eye(128, dtype=BF)
-    ahead = lambda t, s: (jnp.clip(t - 1, 0, planes - 1), 0, 0)
-    done = lambda t, s: (jnp.clip(t - 2, 0, planes - 1), 0, 0)
-    each = lambda t, s: (t, 0, 0)
-    whole = lambda t, s: (0, 0)
+    cube = lambda t, s: (0, 0, 0)
+    flat = lambda t, s: (0, 0)
     return pl.pallas_call(
         tile_kernel,
         out_shape=jax.ShapeDtypeStruct((256, 128, 128), BF),
         grid_spec=pltpu.PrefetchScalarGridSpec(
             num_scalar_prefetch=1,
-            grid=(planes + 2,),
+            grid=(8,),
             in_specs=[
-                pl.BlockSpec((1, 1024, 128), ahead),
-                pl.BlockSpec((1, 1, 1024), ahead),
-                pl.BlockSpec((1, 1, 1024), done),
-                pl.BlockSpec((1, 1, 1024), done),
-                pl.BlockSpec((1, 32, 128), each),
-                pl.BlockSpec((1, 32, 128), each),
-                pl.BlockSpec((1024, 128), whole),
-                pl.BlockSpec((1024, 128), whole),
-                pl.BlockSpec((512, 256), whole),
-                pl.BlockSpec((128, 128), whole),
+                pl.BlockSpec((4, 1024, 128), lambda t, s: (t, 0, 0)),
+                pl.BlockSpec((32, 1, 1024), cube),
+                pl.BlockSpec((32, 1, 1024), cube),
+                pl.BlockSpec((34, 32, 128), cube),
+                pl.BlockSpec((34, 32, 128), cube),
+                pl.BlockSpec((1024, 128), flat),
+                pl.BlockSpec((1024, 128), flat),
+                pl.BlockSpec((512, 256), flat),
             ],
             out_specs=pl.BlockSpec(memory_space=pl.ANY),
             scratch_shapes=[
                 pltpu.VMEM((2, 128, 1280), BF),
                 pltpu.VMEM((2, 128, 1024), BF),
-                pltpu.VMEM((3, 128, 1024), F32),
+                pltpu.VMEM((4, 128, 1024), F32),
                 pltpu.VMEM((2, 4, 128, 128), BF),
                 pltpu.SemaphoreType.DMA((2, 4)),
             ],
         ),
         compiler_params=pltpu.CompilerParams(
-            dimension_semantics=("arbitrary",), vmem_limit_bytes=32 * 2**20
+            dimension_semantics=("arbitrary",), vmem_limit_bytes=60 * 2**20
         ),
         name="galerkin_tiles",
-    )(slots, basis, link, link, diag, before_y, after_y, before_x, after_x, stencil, eye)
-
-
-def factor_kernel(pivot_ref, factor_ref, inverse_ref, work, block):
+    )(slots, basis, link, diag, before_y, after_y, before_x, after_x, stencil)
+
+
+def factor_kernel(pivot_ref, factor_ref, inverse_ref, work):
     size = pivot_ref.shape[0]
     count = size // 128
     rows = lax.broadcasted_iota(jnp.int32, (128, 128), 0)
     lanes = lax.broadcasted_iota(jnp.int32, (128, 128), 1)
-    row_ids = lax.broadcasted_iota(jnp.int32, (128, 1), 0)
-    lane_ids = lax.broadcasted_iota(jnp.int32, (1, 128), 1)
+    sub8 = lax.broadcasted_iota(jnp.int32, (8, 128), 0)
+    lane8 = lax.broadcasted_iota(jnp.int32, (8, 128), 1)
+    all_rows = lax.broadcasted_iota(jnp.int32, (size, 1), 0)
     work[...] = pivot_ref[...]
     factor_ref[...] = jnp.zeros_like(factor_ref)
     inverse_ref[...] = jnp.zeros_like(inverse_ref)
-    for b in range(count):
-        own = slice(128 * b, 128 * b + 128)
-        rest = slice(128 * b + 128, size)
-        block[:, 0:128] = work[own, own]
-        block[:, 128:256] = jnp.where(rows == lanes, 1.0, 0.0)
-
-        def eliminate(j, carry):
-            left = block[:, 0:128]
-            right = block[:, 128:256]
-            pivot_row = block[pl.ds(j, 1), :]
-            pivot = jnp.sum(jnp.where(lane_ids == j, pivot_row[:, 0:128], 0.0), axis=1, keepdims=True)
-            column = jnp.sum(jnp.where(lanes == j, left, 0.0), axis=1, keepdims=True)
-            ratio = jnp.where(row_ids > j, column * (1.0 / pivot), 0.0)
-            block[:, 0:128] = left - ratio * pivot_row[:, 0:128]
-            block[:, 128:256] = right - ratio * pivot_row[:, 128:256]
-            return carry
-
-        lax.fori_loop(0, 128, eliminate, 0)
-        upper = block[:, 0:128]
-        pivots = jnp.sum(jnp.where(rows == lanes, upper, 0.0), axis=1, keepdims=True)
+
+    def one_block(b, carry):
+        own = pl.ds(pl.multiple_of(128 * b, 128), 128)
+        block = work[own, own]
+        parts = [block[8 * i:8 * i + 8] for i in range(16)]
+        for panel in range(16):
+            cols = []
+            for k in range(8):
+                lane = slice(8 * panel + k, 8 * panel + k + 1)
+                cols.append([jnp.broadcast_to(parts[i][:, lane], (8, 128)) for i in range(panel, 16)])
+            for k in range(8):
+                lane = 8 * panel + k
+                pivot_row = jnp.broadcast_to(parts[panel][k:k + 1], (8, 128))
+                pivot_row = jnp.where(lane8 == lane, 1.0, pivot_row)
+                inverse = 1.0 / jnp.broadcast_to(cols[k][0][k:k + 1], (8, 128))
+                heads = [None] * 8
+                for l in range(k + 1, 8):
+                    heads[l] = jnp.broadcast_to(cols[l][0][k:k + 1], (8, 128))
+                for i in range(panel, 16):
+                    ratio = cols[k][i - panel] * inverse
+                    clear = lane8 == lane
+                    if i == panel:
+                        ratio = jnp.where(sub8 > k, ratio, 0.0)
+                        clear = clear & (sub8 > k)
+                    for l in range(k + 1, 8):
+                        cols[l][i - panel] = cols[l][i - panel] - ratio * heads[l]
+                    parts[i] = jnp.where(clear, 0.0, parts[i]) - ratio * pivot_row
+        full = jnp.concatenate(parts, axis=0)
+        pivots = jnp.sum(jnp.where(rows == lanes, full, 0.0), axis=1, keepdims=True)
         scale = 1.0 / jnp.sqrt(pivots)
-        upper = jnp.where(rows <= lanes, upper * scale, 0.0)
-        inverse = jnp.where(rows >= lanes, block[:, 128:256] * scale, 0.0)
+        upper = jnp.where(rows <= lanes, full * scale, 0.0)
+        inv = jnp.where(rows > lanes, full * scale, jnp.where(rows == lanes, scale, 0.0))
+        below = dot32(work[:, own], inv, NT)
+        below = jnp.where(all_rows >= 128 * b + 128, below, 0.0)
+        factor_ref[:, own] = below
         factor_ref[own, own] = upper.T
-        inverse_ref[own, own] = inverse
-        if b + 1 < count:
-            below = dot32(work[rest, own], inverse, NT)
-            factor_ref[rest, own] = below
-            work[rest, rest] = work[rest, rest] - dot32(below, below, NT)
+        inverse_ref[own, own] = inv
+        work[...] = work[...] - dot32(below, below, NT)
+        return carry
+
+    lax.fori_loop(0, count, one_block, 0)
     for b in range(1, count):
         own = slice(128 * b, 128 * b + 128)
         left = slice(0, 128 * b)
@@ -184,7 +207,7 @@
         out_shape=[jax.ShapeDtypeStruct((size, size), F32)] * 2,
         in_specs=[pl.BlockSpec(memory_space=pltpu.VMEM)],
         out_specs=[pl.BlockSpec(memory_space=pltpu.VMEM)] * 2,
-        scratch_shapes=[pltpu.VMEM((size, size), F32), pltpu.VMEM((128, 256), F32)],
+        scratch_shapes=[pltpu.VMEM((size, size), F32)],
         compiler_params=pltpu.CompilerParams(vmem_limit_bytes=32 * 2**20),
         cost_estimate=pl.CostEstimate(flops=10**10, bytes_accessed=3 * 2**20, transcendentals=0),
         name="pivot_factor",
@@ -250,7 +273,7 @@
             scratch_shapes=[pltpu.VMEM((128, 128, 128), F32)],
         ),
         compiler_params=pltpu.CompilerParams(
-            dimension_semantics=("arbitrary",), vmem_limit_bytes=48 * 2**20
+            dimension_semantics=("arbitrary",), vmem_limit_bytes=60 * 2**20
         ),
         name="trailing_front",
     )(place, panel_rows, panel_cols, base, received)
@@ -617,19 +640,13 @@
         base_front,
     )
 
-    listed = block_lists.reshape(devices, 128, 2)
-    row_block = listed[:, :, 0]
-    col_block = listed[:, :, 1]
-    owner_ids = row_block // members * members + col_block // groups
-    local_block = row_block % members * groups + col_block % groups
-    own_owner = lax.dynamic_index_in_dim(owner_ids, me, 0, keepdims=False)
+    own_list = lax.dynamic_index_in_dim(block_lists.reshape(devices, 128, 2), me, 0, keepdims=False)
+    own_owner = own_list[:, 0] // members * members + own_list[:, 1] // groups
     order = jnp.arange(128)
     rank = jnp.sum(
         (own_owner[:, None] == own_owner[None, :]) & (order[None, :] < order[:, None]), axis=1
     )
     slots = (own_owner * 2 + rank).astype(jnp.int32)
-    place = arrivals(owner_ids, local_block, me)
-    panel_place = arrivals(owner_ids, local_block, group * members)
 
     outgoing = galerkin_tiles(
         slots,
@@ -642,7 +659,18 @@
         after_x,
     )
 
-    outgoing, lead = lax.optimization_barrier((outgoing, lead))
+    outgoing, lead, block_lists = lax.optimization_barrier((outgoing, lead, block_lists))
+    listed = block_lists.reshape(devices, 128, 2)
+    row_block = listed[:, :, 0]
+    col_block = listed[:, :, 1]
+    owner_ids = row_block // members * members + col_block // groups
+    local_block = row_block % members * groups + col_block % groups
+    place = arrivals(owner_ids, local_block, me)
+    panel_place = arrivals(owner_ids, local_block, group * members)
+    lead = lead.astype(F32)
+    symmetric = jnp.tril(lead) + jnp.tril(lead, -1).T
+    pivot_matrix = symmetric + jnp.diag(jnp.sum(jnp.abs(symmetric), axis=1) + 1.0)
+    factor, inverse = pivot_factor(pivot_matrix)
     strips = outgoing.reshape(groups, members, 2, 128, 128)[:, 0]
     strips = strips.reshape(groups, 2, members, 4, 128).transpose(0, 2, 1, 3, 4)
     strips = strips.reshape(devices, 2, 4, 128)
@@ -651,6 +679,7 @@
         outgoing.reshape(devices, 2, 128, 128), ("grp", "sub"), split_axis=0, concat_axis=0, tiled=True
     ).reshape(256, 128, 128)
 
+    strips, inverse = lax.optimization_barrier((strips, inverse))
     strips = jnp.where((panel_place >= 0)[:, None], strips.reshape(256, 512), 0)
     pick = (panel_place[None, :] == jnp.arange(128)[:, None]).astype(BF)
     strips = dotb(pick, strips, NN).reshape(members, groups, 4, 128)
@@ -658,10 +687,6 @@
     strips = lax.all_to_all(strips, "sub", split_axis=0, concat_axis=0, tiled=True)
     front_rows = base_rows.astype(F32) + strips.reshape(128, 512)
 
-    lead = lead.astype(F32)
-    symmetric = jnp.tril(lead) + jnp.tril(lead, -1).T
-    pivot_matrix = symmetric + jnp.diag(jnp.sum(jnp.abs(symmetric), axis=1) + 1.0)
-    factor, inverse = pivot_factor(pivot_matrix)
     solved = dot32(front_rows, inverse, NT)
     in_lead = (group == 0) & (member < 4)
     own_factor = lax.dynamic_slice_in_dim(factor, 128 * jnp.minimum(member, 3), 128, 0)

time: 328 us -> 315 us (0.960)
  Pallas kernels: 246 us -> 239 us
  waiting for transfers between devices: 6.27 us -> 0.01 us
    pallas_call x1, Pallas kernels: 85 us -> 146 us  [panel_spread(): pl.pallas_call(panel_kernel, out_shape=[jax.ShapeDtypeStruct((4096, 512),...]
    pallas_call x1, Pallas kernels: 59.7 us -> 25 us  [galerkin_tiles(): pl.pallas_call(tile_kernel, out_shape=jax.ShapeDtypeStruct((256, 128, 128...]
    pallas_call x1, Pallas kernels: 59.4 us -> 25 us  [pivot_factor(): pl.pallas_call(factor_kernel, out_shape=[jax.ShapeDtypeStruct((size, size...]
    all_to_all x1, waiting for transfers between devices: 6.27 us -> 0.01 us  [per_device(): lax.all_to_all(strips, ('grp', 'sub'), split_axis=0, concat_axis=0, tiled...]
    unnamed x15 -> x20, local copies, waits for them, and re-layouts: 14 us -> 8.68 us
  transfers between devices with their start and end apart: 2 -> 2, of which waited for: 1 -> 0; matrix products, arithmetic and copies ran while one was open for 1% -> 1% of each run, Pallas kernels for 44% -> 54%
where the time goes in v3:
time: 315 us; the launch traced here: 314 us
  Pallas kernels  239 us (76%)
  starting transfers between devices  32.9 us (10%)
  local copies, waits for them, and re-layouts  21.1 us (7%)
  blocking collectives  14.3 us (5%)
  other arithmetic  4.48 us (1%)
    pallas_call x1, Pallas kernels, panel_spread(): pl.pallas_call(panel_kernel, out_shape=[jax.ShapeDtypeStruct((4096, 512),...  146 us
    pallas_call x1, Pallas kernels, galerkin_tiles(): pl.pallas_call(tile_kernel, out_shape=jax.ShapeDtypeStruct((256, 128, 128...  25 us
    pallas_call x1, Pallas kernels, pivot_factor(): pl.pallas_call(factor_kernel, out_shape=[jax.ShapeDtypeStruct((size, size...  25 us
    pallas_call x1, Pallas kernels, opening(): pl.pallas_call(opening_kernel, out_shape=[jax.ShapeDtypeStruct((1024, 128...  24.9 us
    all_to_all x1, starting transfers between devices, per_device(): lax.all_to_all(strips, ('grp', 'sub'), split_axis=0, concat_axis=0, tiled...  24.5 us
    pallas_call x1, Pallas kernels, trailing_front(): pl.pallas_call(final_kernel, out_shape=jax.ShapeDtypeStruct((4096, 512),...  18.7 us
    all_to_all x1, blocking collectives, per_device(): lax.all_to_all(strips, 'sub', split_axis=0, concat_axis=0, tiled=True)  14.3 us
    unnamed x20, local copies, waits for them, and re-layouts  8.68 us
  transfers between devices with their start and end apart: 2, of which 0 were waited for; matrix products, arithmetic and copies ran while one was open for 1% of the time, Pallas kernels for 54%

profile of v3, /device:TPU:121, one launch (start us, length us, event | category | flops | bytes accessed | tf_op | source)
XLA Modules:
  0.0 314.2 jit_solution(7369019739122995763)
XLA Ops:
  0.7 1.1 slice_reduce_fusion
  1.7 0.7 fusion.45
  2.5 0.9 copy.70
  3.4 2.0 reshape.275.link_ref
  5.4 1.1 fusion.43
  6.5 1.1 fusion.44
  7.5 0.1 mul.84
  7.6 0.1 mul.81
  7.7 0.1 mul.78
  7.7 0.1 mul.75
  7.8 2.0 reshape.276.diag_ref
  9.8 0.2 convert_reduce_fusion
  9.9 0.6 multiply_add_fusion.1.slot_ref
  10.5 1.0 fusion.6.stencil_ref
  11.5 0.3 fusion.1
  11.8 0.3 fusion.3
  12.2 0.0 copy-start
  12.2 2.2 copy-done
  14.4 24.9 %opening.1 = (bf16[1024,128]{1,0:T(8,128)(2,1)S(1)}, bf16[1024,128]{1,0:T(8,128)(2,1)S(1)}, bf16[1088,128]{1,0:T(8,128)(2,1)S(1)}, bf16[1088,128]{1,0:T(8,128)(2...) custom-call(bf16[1024,128]{1,0:T(8,128)(2,1)S(1)} %get-tuple-element.56.high_x, ...), custom_call_target="tpu_custom_call" | custom-call | tf_op jit(solution)/shard_map/opening/pallas_call | solution.py:454
  39.3 0.0 copy-start.4
  39.3 0.7 copy-done.4
  40.0 0.0 copy-start.5
  40.0 0.7 copy-done.5
  40.7 0.0 copy-start.6
  40.7 0.7 copy-done.6
  41.3 0.0 copy-start.7
  41.4 0.7 copy-done.7
  42.1 0.0 copy-start.8
  42.1 25.0 %galerkin_tiles.1 = bf16[256,128,128]{2,1,0:T(8,128)(2,1)} custom-call(s32[128]{0:T(128)} %multiply_add_fusion.1.slot_ref, bf16[32,1024,128]{2,1,0:T(8,128)(2,1)} %bitcast.138, f32[32,1,1024]{2,1,0:T(1,128)} %reshape.275.link_ref, f32[32,1,1024]{2,1,0:T(1,128)} %reshape.276.diag_ref, bf16[34,32,128]{2,1,0:T(8,128)(2,1)} %bitcast.134, ...), custom_call_target="tpu_custom_call" | custom-call | tf_op jit(solution)/shard_map/galerkin_tiles/pallas_call | solution.py:112
  67.1 1.0 slice.54
  68.1 0.9 copy.53
  69.0 24.5 %all-to-all-start = ((bf16[128,2,4,128]{3,2,1,0:T(4,128)(2,1)}), bf16[128,2,4,128]{3,2,1,0:T(4,128)(2,1)}, u32[]{:S(2)}, u32[]{:S(2)}) async-start(bf16[128,2,4,128]{3,2,1,0:T(4,128)(2,1)} %copy.53), calls=%async_computation | async-start | bytes 524288 | tf_op jit(solution)/shard_map/all_to_all | solution.py:677
  93.5 0.0 copy-done.8
  93.6 0.2 select_reduce_fusion.5
  93.8 0.1 select_reduce_fusion.2
  93.9 0.2 copy.46
  94.1 0.2 copy.48
  94.3 0.3 abs_reduce_fusion
  94.6 0.3 copy.49
  95.0 0.1 select_add_fusion.pivot_ref
  95.1 25.0 %pivot_factor.1 = (f32[512,512]{1,0:T(8,128)S(1)}, f32[512,512]{1,0:T(8,128)S(1)}) custom-call(f32[512,512]{1,0:T(8,128)S(1)} %select_add_fusion.pivot_ref), custom_call_target="tpu_custom_call" | custom-call | flops 10000000000 | bytes 3145728 | tf_op jit(solution)/shard_map/pivot_factor/pallas_call | solution.py:205
  120.1 0.2 select_reduce_fusion.1
  120.4 0.1 copy.50
  120.5 0.1 eq.103
  120.6 0.0 all-to-all-done
  120.6 1.1 fusion.7
  121.7 0.1 copy.58
  121.8 0.2 convolution_bitcast_fusion
  122.1 0.2 copy.59
  122.2 0.2 reshape.294
  122.4 14.3 %all_to_all.15 = f32[32,4,512]{2,1,0:T(4,128)S(1)} all-to-all(f32[32,4,512]{2,1,0:T(4,128)S(1)} %reshape.294), channel_id=1, replica_groups=mesh['grp'=4,'sub'=32] {'sub'}, dimensions={0} | all-to-all | bytes 524288 | tf_op jit(solution)/shard_map/all_to_all | solution.py:687
  136.7 8.4 %all-to-all-start.2 = ((bf16[128,2,128,128]{3,2,1,0:T(8,128)(2,1)}), bf16[128,2,128,128]{3,2,1,0:T(8,128)(2,1)}, u32[]{:S(2)}, u32[]{:S(2)}) async-start(bf16[128,2,128,128]{3,2,1,0:T(8,128)(2,1)} %bitcast.137), calls=%async_computation.2 | async-start | bytes 16777216 | tf_op jit(solution)/shard_map/all_to_all | solution.py:678
  145.1 0.1 copy.45
  145.2 0.7 reshape.280.place_ref
  145.9 0.1 reshape.285
  146.0 1.1 fusion.panel_ref
  147.2 0.0 copy-start.3
  147.2 145.6 %panel_spread.1 = (bf16[4096,512]{1,0:T(8,128)(2,1)S(1)}, bf16[512,512]{1,0:T(8,128)(2,1)S(1)}) custom-call(bf16[128,512]{1,0:T(8,128)(2,1)S(1)} %fusion.panel_ref), custom_call_target="tpu_custom_call" | custom-call | tf_op jit(solution)/shard_map/panel_spread/pallas_call | solution.py:602
  292.7 0.0 copy-start.1
  292.7 2.0 copy-done.1
  294.7 0.8 copy-done.2
  295.5 0.0 all-to-all-done.2
  295.5 18.7 %trailing_front.1 = f32[4096,512]{1,0:T(8,128)} custom-call(s32[256]{0:T(256)} %reshape.280.place_ref, bf16[4096,512]{1,0:T(8,128)(2,1)} %copy-done.1, bf16[512,512]{1,0:T(8,128)(2,1)} %copy-done.2, bf16[4096,512]{1,0:T(8,128)(2,1)} %base_ref.3, bf16[256,128,128]{2,1,0:T(8,128)(2,1)} %bitcast.29.received_ref), custom_call_target="tpu_custom_call" | custom-call | tf_op jit(solution)/shard_map/trailing_front/pallas_call | solution.py:260
  314.2 0.0 copy-done.3
  (14 shorter events, 0.1 us)
Async XLA Ops:
  12.2 2.2 copy-start
  39.3 0.7 copy-start.4
  40.0 0.7 copy-start.5
  40.7 0.7 copy-start.6
  41.3 0.7 copy-start.7
  42.1 51.5 %copy-start.8 = (s32[16384,2]{0,1:T(2,128)S(1)}, s32[16384,2]{0,1:T(2,128)}, u32[]{:S(2)}) copy-start(s32[16384,2]{0,1:T(2,128)} %param.9) | copy-start | bytes 393220
  69.0 51.6 %all-to-all-start = ((bf16[128,2,4,128]{3,2,1,0:T(4,128)(2,1)}), bf16[128,2,4,128]{3,2,1,0:T(4,128)(2,1)}, u32[]{:S(2)}, u32[]{:S(2)}) async-start(bf16[128,2,4,128]{3,2,1,0:T(4,128)(2,1)} %copy.53), calls=%async_computation | async-start | bytes 524288 | tf_op jit(solution)/shard_map/all_to_all | solution.py:677
  136.7 158.8 %all-to-all-start.2 = ((bf16[128,2,128,128]{3,2,1,0:T(8,128)(2,1)}), bf16[128,2,128,128]{3,2,1,0:T(8,128)(2,1)}, u32[]{:S(2)}, u32[]{:S(2)}) async-start(bf16[128,2,128,128]{3,2,1,0:T(8,128)(2,1)} %bitcast.137), calls=%async_computation.2 | async-start | bytes 16777216 | tf_op jit(solution)/shard_map/all_to_all | solution.py:678
  147.2 167.1 %copy-start.3 = (bf16[128,512]{1,0:T(8,128)(2,1)}, bf16[128,512]{1,0:T(8,128)(2,1)S(1)}, u32[]{:S(2)}) copy-start(bf16[128,512]{1,0:T(8,128)(2,1)S(1)} %fusion.panel_ref) | copy-start | bytes 393220
  292.7 2.0 copy-start.1
  294.7 0.8 copy-start.2

commit v4 on v3

--- a/solution.py
+++ b/solution.py
@@ -7,6 +7,7 @@
 from jax.experimental.pallas import tpu as pltpu
 from jax.sharding import PartitionSpec as P
 
+EARLY = 13
 NT = (((1,), (1,)), ((), ()))
 NN = (((1,), (0,)), ((), ()))
 BF = jnp.bfloat16
@@ -24,7 +25,7 @@
 def tile_kernel(
     slot_ref, basis_ref, link_ref, diag_ref, before_y_ref, after_y_ref,
     before_x_ref, after_x_ref, stencil_ref, out_ref,
-    scaled_t, basis_t, partial, stage, sems,
+    scaled_t, basis_t, partial, stage, sems, clear_sems,
 ):
     step = pl.program_id(0)
     gap = jnp.zeros((96, 128), BF)
@@ -65,8 +66,18 @@
             tail = (image - head.astype(F32)).astype(BF)
             stage[slot, q] = (dotb(own, head, NT) + dotb(own, tail, NT)).astype(BF)
 
+    def clear(n):
+        return pltpu.make_async_copy(
+            stage.at[0, 0], out_ref.at[64 * (n // 2) + n % 2], clear_sems.at[n]
+        )
+
     @pl.when(step == 0)
     def _():
+        stage[0, 0] = jnp.zeros((128, 128), BF)
+        for n in range(8):
+            clear(n).start()
+        for n in range(8):
+            clear(n).wait()
         sides(1, -1)
         scaled_t[1, :, 128:1152] = before_x_ref[...].T
         spread(1, 3)
@@ -132,6 +143,7 @@
                 pltpu.VMEM((4, 128, 1024), F32),
                 pltpu.VMEM((2, 4, 128, 128), BF),
                 pltpu.SemaphoreType.DMA((2, 4)),
+                pltpu.SemaphoreType.DMA((8,)),
             ],
         ),
         compiler_params=pltpu.CompilerParams(
@@ -209,7 +221,6 @@
         out_specs=[pl.BlockSpec(memory_space=pltpu.VMEM)] * 2,
         scratch_shapes=[pltpu.VMEM((size, size), F32)],
         compiler_params=pltpu.CompilerParams(vmem_limit_bytes=32 * 2**20),
-        cost_estimate=pl.CostEstimate(flops=10**10, bytes_accessed=3 * 2**20, transcendentals=0),
         name="pivot_factor",
     )(pivot_matrix)
 
@@ -384,7 +395,7 @@
             base_copy(m).start()
             return carry
 
-        lax.fori_loop(1, members, send, 0)
+        lax.fori_loop(1, EARLY, send, 0)
 
     @pl.when(root)
     def _():
@@ -440,10 +451,10 @@
             base_copy(m).wait_send()
             return carry
 
-        lax.fori_loop(1, members, sent, 0)
+        lax.fori_loop(1, EARLY, sent, 0)
         own_rows.wait()
 
-    @pl.when(member > 0)
+    @pl.when((member > 0) & (member < EARLY))
     def _():
         base_copy(member).wait_recv()
 
@@ -473,6 +484,178 @@
     )(high_x, low_x, high_y, low_y, base_front)
 
 
+def front_kernel(
+    key_ref, tiles_ref, base_front_ref, early_ref, front_ref, strips, sums, added, late,
+    strip_send, strip_recv, sum_send, sum_recv, base_send, base_recv, own_sem,
+):
+    groups, members, devices, parts, base = 4, 32, 128, 8, 8
+    group = lax.axis_index("grp")
+    member = lax.axis_index("sub")
+    me = group * members + member
+    takes = (member >= base) & (member < base + parts)
+    barrier = pltpu.get_barrier_semaphore()
+
+    def greet(d, carry):
+        other = lax.rem(me + d, devices)
+        pl.semaphore_signal(barrier, 1, device_id=at(other // members, lax.rem(other, members)))
+        return carry
+
+    lax.fori_loop(1, devices, greet, 0)
+    pl.semaphore_wait(barrier, devices - 1)
+
+    def source(g, r):
+        first = pl.ds(2 * members * g, 2)
+        return tiles_ref.at[first, pl.ds(pl.multiple_of(16 * r, 16), 16)]
+
+    def strip_copy(sender, g, r, k):
+        return pltpu.make_async_remote_copy(
+            source(g, r), strips.at[pl.ds(2 * sender, 2)], strip_send.at[k], strip_recv.at[sender],
+            device_id=at(g, base + r),
+        )
+
+    own_rank = lax.rem(member, parts)
+    own_strip = pltpu.make_async_copy(
+        source(group, own_rank), strips.at[pl.ds(2 * me, 2)], own_sem.at[0]
+    )
+
+    def target(j):
+        t = lax.rem(j + group * parts + own_rank, groups * parts)
+        return t // parts, lax.rem(t, parts)
+
+    def start_strip(j, carry):
+        g, r = target(j)
+
+        @pl.when((g != group) | (base + r != member))
+        def _():
+            strip_copy(me, g, r, j).start()
+
+        return carry
+
+    lax.fori_loop(0, groups * parts, start_strip, 0)
+
+    def base_copy(m):
+        rows = pl.ds(pl.multiple_of(128 * m, 128), 128)
+        return pltpu.make_async_remote_copy(
+            base_front_ref.at[rows], late, base_send.at[m], base_recv, device_id=at(group, m)
+        )
+
+    @pl.when(member == 0)
+    def _():
+        def send(m, carry):
+            base_copy(m).start()
+            return carry
+
+        lax.fori_loop(EARLY, members, send, 0)
+
+    def sum_copy(r, a):
+        rows = pl.ds(pl.multiple_of(16 * r, 16), 16)
+        return pltpu.make_async_remote_copy(
+            sums.at[pl.ds(4 * a, 4)], added.at[:, rows], sum_send.at[a], sum_recv.at[r],
+            device_id=at(group, a),
+        )
+
+    own_sum = pltpu.make_async_copy(
+        sums.at[pl.ds(4 * member, 4)],
+        added.at[:, pl.ds(pl.multiple_of(16 * own_rank, 16), 16)],
+        own_sem.at[1],
+    )
+
+    @pl.when(takes)
+    def _():
+        own_strip.start()
+
+        def arrive(d, carry):
+            strip_copy(lax.rem(me + d, devices), group, own_rank, 0).wait_recv()
+            return carry
+
+        lax.fori_loop(1, devices, arrive, 0)
+        own_strip.wait()
+        rows = strips[...].reshape(4096, 128)
+        for n in range(8):
+            ids = 256 * n + lax.broadcasted_iota(jnp.int32, (256, 4096), 0)
+            pick = jnp.where(key_ref[...] == ids, 1.0, 0.0).astype(BF)
+            sums[16 * n:16 * n + 16] = dotb(pick, rows, NN).astype(BF).reshape(16, 16, 128)
+
+        def send(d, carry):
+            sum_copy(own_rank, lax.rem(member + d, members)).start()
+            return carry
+
+        lax.fori_loop(1, members, send, 0)
+        own_sum.start()
+
+    for r in range(parts):
+        @pl.when(member != base + r)
+        def _():
+            sum_copy(r, member).wait_recv()
+
+    @pl.when(takes)
+    def _():
+        own_sum.wait()
+
+    @pl.when(member < EARLY)
+    def _():
+        for q in range(4):
+            cols = slice(128 * q, 128 * q + 128)
+            front_ref[:, cols] = early_ref[:, cols].astype(F32) + added[q].astype(F32)
+
+    @pl.when(member >= EARLY)
+    def _():
+        base_copy(member).wait_recv()
+        for q in range(4):
+            cols = slice(128 * q, 128 * q + 128)
+            front_ref[:, cols] = late[:, cols].astype(F32) + added[q].astype(F32)
+
+    def sent_strip(j, carry):
+        g, r = target(j)
+
+        @pl.when((g != group) | (base + r != member))
+        def _():
+            strip_copy(me, g, r, j).wait_send()
+
+        return carry
+
+    lax.fori_loop(0, groups * parts, sent_strip, 0)
+
+    @pl.when(takes)
+    def _():
+        def sent(d, carry):
+            sum_copy(own_rank, lax.rem(member + d, members)).wait_send()
+            return carry
+
+        lax.fori_loop(1, members, sent, 0)
+
+    @pl.when(member == 0)
+    def _():
+        def sent(m, carry):
+            base_copy(m).wait_send()
+            return carry
+
+        lax.fori_loop(EARLY, members, sent, 0)
+
+
+def front_rows_of(key, tiles, base_front, early):
+    dma = pltpu.SemaphoreType.DMA
+    anywhere = pl.BlockSpec(memory_space=pl.ANY)
+    vmem = pl.BlockSpec(memory_space=pltpu.VMEM)
+    return pl.pallas_call(
+        front_kernel,
+        out_shape=jax.ShapeDtypeStruct((128, 512), F32),
+        in_specs=[vmem, anywhere, anywhere, vmem],
+        out_specs=vmem,
+        scratch_shapes=[
+            pltpu.VMEM((256, 16, 128), BF),
+            pltpu.VMEM((128, 16, 128), BF),
+            pltpu.VMEM((4, 128, 128), BF),
+            pltpu.VMEM((128, 512), BF),
+            dma((32,)), dma((128,)), dma((32,)), dma((8,)), dma((32,)), dma, dma((2,)),
+        ],
+        compiler_params=pltpu.CompilerParams(
+            collective_id=2, has_side_effects=True, vmem_limit_bytes=60 * 2**20
+        ),
+        name="front_rows",
+    )(key, tiles, base_front, early)
+
+
 def panel_kernel(
     panel_ref, rows_ref, cols_ref, send, recv, fold_send, fold_recv, col_send, col_recv, own_sem
 ):
@@ -659,34 +842,26 @@
         after_x,
     )
 
-    outgoing, lead, block_lists = lax.optimization_barrier((outgoing, lead, block_lists))
     listed = block_lists.reshape(devices, 128, 2)
     row_block = listed[:, :, 0]
     col_block = listed[:, :, 1]
     owner_ids = row_block // members * members + col_block // groups
     local_block = row_block % members * groups + col_block % groups
+    panel_place = arrivals(owner_ids, local_block, group * members)
+    key = jnp.where(panel_place[:, None] < 0, -1, panel_place[:, None] * 16 + jnp.arange(16)[None, :])
+    front_rows = front_rows_of(key.reshape(1, 4096), outgoing, base_front, base_rows)
+
+    outgoing, lead, front_rows, owner_ids, local_block = lax.optimization_barrier(
+        (outgoing, lead, front_rows, owner_ids, local_block)
+    )
+    received = lax.all_to_all(
+        outgoing.reshape(devices, 2, 128, 128), ("grp", "sub"), split_axis=0, concat_axis=0, tiled=True
+    ).reshape(256, 128, 128)
     place = arrivals(owner_ids, local_block, me)
-    panel_place = arrivals(owner_ids, local_block, group * members)
     lead = lead.astype(F32)
     symmetric = jnp.tril(lead) + jnp.tril(lead, -1).T
     pivot_matrix = symmetric + jnp.diag(jnp.sum(jnp.abs(symmetric), axis=1) + 1.0)
     factor, inverse = pivot_factor(pivot_matrix)
-    strips = outgoing.reshape(groups, members, 2, 128, 128)[:, 0]
-    strips = strips.reshape(groups, 2, members, 4, 128).transpose(0, 2, 1, 3, 4)
-    strips = strips.reshape(devices, 2, 4, 128)
-    strips = lax.all_to_all(strips, ("grp", "sub"), split_axis=0, concat_axis=0, tiled=True)
-    received = lax.all_to_all(
-        outgoing.reshape(devices, 2, 128, 128), ("grp", "sub"), split_axis=0, concat_axis=0, tiled=True
-    ).reshape(256, 128, 128)
-
-    strips, inverse = lax.optimization_barrier((strips, inverse))
-    strips = jnp.where((panel_place >= 0)[:, None], strips.reshape(256, 512), 0)
-    pick = (panel_place[None, :] == jnp.arange(128)[:, None]).astype(BF)
-    strips = dotb(pick, strips, NN).reshape(members, groups, 4, 128)
-    strips = strips.transpose(0, 2, 1, 3).reshape(members, 4, 512)
-    strips = lax.all_to_all(strips, "sub", split_axis=0, concat_axis=0, tiled=True)
-    front_rows = base_rows.astype(F32) + strips.reshape(128, 512)
-
     solved = dot32(front_rows, inverse, NT)
     in_lead = (group == 0) & (member < 4)
     own_factor = lax.dynamic_slice_in_dim(factor, 128 * jnp.minimum(member, 3), 128, 0)

time: 315 us -> 289 us (0.917)
  starting transfers between devices: 32.9 us -> 9.66 us
  blocking collectives: 14.3 us -> 0 us
  Pallas kernels: 239 us -> 252 us
    pallas_call x0 -> x1, Pallas kernels: none -> 39.2 us  [front_rows_of(): pl.pallas_call(front_kernel, out_shape=jax.ShapeDtypeStruct((128, 512), F...]
    pallas_call x1, Pallas kernels: 146 us -> 119 us  [panel_spread(): pl.pallas_call(panel_kernel, out_shape=[jax.ShapeDtypeStruct((4096, 512),...]
    all_to_all x1 -> x0, starting transfers between devices: 24.5 us -> none  [per_device(): lax.all_to_all(strips, ('grp', 'sub'), split_axis=0, concat_axis=0, tiled...]
    all_to_all x1 -> x0, blocking collectives: 14.3 us -> none  [per_device(): lax.all_to_all(strips, 'sub', split_axis=0, concat_axis=0, tiled=True)]
    unnamed x20 -> x21, local copies, waits for them, and re-layouts: 8.68 us -> 9.33 us
  transfers between devices with their start and end apart: 2 -> 1, of which waited for: 0 -> 0; matrix products, arithmetic and copies ran while one was open for 1% -> 1% of each run, Pallas kernels for 54% -> 50%
where the time goes in v4:
time: 289 us; the launch traced here: 288 us
  Pallas kernels  252 us (87%)
  local copies, waits for them, and re-layouts  20.3 us (7%)
  starting transfers between devices  9.66 us (3%)
  other arithmetic  3.77 us (1%)
    pallas_call x1, Pallas kernels, panel_spread(): pl.pallas_call(panel_kernel, out_shape=[jax.ShapeDtypeStruct((4096, 512),...  119 us
    pallas_call x1, Pallas kernels, front_rows_of(): pl.pallas_call(front_kernel, out_shape=jax.ShapeDtypeStruct((128, 512), F...  39.2 us
    pallas_call x1, Pallas kernels, galerkin_tiles(): pl.pallas_call(tile_kernel, out_shape=jax.ShapeDtypeStruct((256, 128, 128...  25.6 us
    pallas_call x1, Pallas kernels, pivot_factor(): pl.pallas_call(factor_kernel, out_shape=[jax.ShapeDtypeStruct((size, size...  25 us
    pallas_call x1, Pallas kernels, opening(): pl.pallas_call(opening_kernel, out_shape=[jax.ShapeDtypeStruct((1024, 128...  24.9 us
    pallas_call x1, Pallas kernels, trailing_front(): pl.pallas_call(final_kernel, out_shape=jax.ShapeDtypeStruct((4096, 512),...  18.7 us
    all_to_all x1, starting transfers between devices, per_device(): lax.all_to_all(outgoing.reshape(devices, 2, 128, 128), ('grp', 'sub'), sp...  9.66 us
    unnamed x21, local copies, waits for them, and re-layouts  9.33 us
  transfers between devices with their start and end apart: 1, of which 0 were waited for; matrix products, arithmetic and copies ran while one was open for 1% of the time, Pallas kernels for 50%

profile of v4, /device:TPU:121, one launch (start us, length us, event | category | flops | bytes accessed | tf_op | source)
XLA Modules:
  0.0 288.0 jit_solution(3748877200558422589)
XLA Ops:
  0.7 1.1 slice_reduce_fusion
  1.7 0.7 fusion.39
  2.5 0.9 copy.28
  3.4 0.2 select_reduce_fusion.5
  3.6 0.2 select_reduce_fusion.4
  3.8 2.0 reshape.286.link_ref
  5.8 1.1 fusion.37
  6.9 1.1 fusion.38
  7.9 0.1 mul.98
  8.0 0.1 mul.95
  8.1 0.1 mul.92
  8.2 0.1 mul.89
  8.2 1.9 reshape.287.diag_ref
  10.2 0.2 convert_reduce_fusion
  10.3 0.6 multiply_add_fusion.slot_ref
  10.9 0.1 copy.18
  11.1 0.1 lt.81
  11.2 0.1 copy.19
  11.3 0.1 mul.105
  11.5 0.1 add_select_fusion
  11.6 0.7 select_n.162.key_ref
  12.3 1.0 fusion.6.stencil_ref
  13.3 0.3 fusion.1
  13.7 0.3 fusion.3
  14.0 0.0 copy-start
  14.0 2.2 copy-done
  16.2 24.9 %opening.1 = (bf16[1024,128]{1,0:T(8,128)(2,1)S(1)}, bf16[1024,128]{1,0:T(8,128)(2,1)S(1)}, bf16[1088,128]{1,0:T(8,128)(2,1)S(1)}, bf16[1088,128]{1,0:T(8,128)(2...) custom-call(bf16[1024,128]{1,0:T(8,128)(2,1)S(1)} %get-tuple-element.55.high_x, ...), custom_call_target="tpu_custom_call" | custom-call | tf_op jit(solution)/shard_map/opening/pallas_call | solution.py:465
  41.1 0.0 copy-start.4
  41.1 0.7 copy-done.4
  41.8 0.0 copy-start.5
  41.8 0.7 copy-done.5
  42.5 0.0 copy-start.6
  42.5 0.7 copy-done.6
  43.2 0.0 copy-start.7
  43.2 0.7 copy-done.7
  43.9 0.0 copy-start.8
  43.9 0.6 copy-done.8
  44.6 25.6 %galerkin_tiles.1.tiles_ref = bf16[256,128,128]{2,1,0:T(8,128)(2,1)} custom-call(s32[128]{0:T(128)} %multiply_add_fusion.slot_ref, bf16[32,1024,128]{2,1,0:T(8,128)(2,1)} %bitcast.108, f32[32,1,1024]{2,1,0:T(1,128)} %reshape.286.link_ref, f32[32,1,1024]{2,1,0:T(1,128)} %reshape.287.diag_ref, bf16[34,32,128]{2,1,0:T(8,128)(2,1)} %bitcast.105, ...), custom_call_target="tpu_custom_call" | custom-call | tf_op jit(solution)/shard_map/galerkin_tiles/pallas_call | solution.py:123
  70.2 39.2 %front_rows.1 = f32[128,512]{1,0:T(8,128)} custom-call(s32[1,4096]{1,0:T(1,128)} %select_n.162.key_ref, bf16[256,128,128]{2,1,0:T(8,128)(2,1)} %galerkin_tiles.1.tiles_ref, bf16[4096,512]{1,0:T(8,128)(2,1)} %base_ref.3, bf16[128,512]{1,0:T(8,128)(2,1)} %copy-done.8), custom_call_target="tpu_custom_call" | custom-call | tf_op jit(solution)/shard_map/front_rows/pallas_call | solution.py:640
  109.4 9.7 %all-to-all-start = ((bf16[128,2,128,128]{3,2,1,0:T(8,128)(2,1)}), bf16[128,2,128,128]{3,2,1,0:T(8,128)(2,1)}, u32[]{:S(2)}, u32[]{:S(2)}) async-start(bf16[128,2,128,128]{3,2,1,0:T(8,128)(2,1)} %bitcast.107), calls=%async_computation | async-start | bytes 16777216 | tf_op jit(solution)/shard_map/all_to_all | solution.py:857
  119.1 0.0 copy-start.9
  119.1 0.1 select_reduce_fusion.2
  119.2 0.2 select_reduce_fusion.1
  119.4 0.1 copy.20
  119.6 0.7 reshape.290.place_ref
  120.2 0.2 copy.21
  120.5 0.2 copy.23
  120.7 0.3 abs_reduce_fusion
  121.0 0.3 copy.24
  121.3 0.1 select_add_fusion.pivot_ref
  121.5 25.0 %pivot_factor.1 = (f32[512,512]{1,0:T(8,128)S(1)}, f32[512,512]{1,0:T(8,128)S(1)}) custom-call(f32[512,512]{1,0:T(8,128)S(1)} %select_add_fusion.pivot_ref), custom_call_target="tpu_custom_call" | custom-call | tf_op jit(solution)/shard_map/pivot_factor/pallas_call | solution.py:217
  146.5 0.0 copy-done.9
  146.5 1.2 fusion.panel_ref
  147.7 0.0 copy-start.3
  147.7 118.8 %panel_spread.1 = (bf16[4096,512]{1,0:T(8,128)(2,1)S(1)}, bf16[512,512]{1,0:T(8,128)(2,1)S(1)}) custom-call(bf16[128,512]{1,0:T(8,128)(2,1)S(1)} %fusion.panel_ref), custom_call_target="tpu_custom_call" | custom-call | tf_op jit(solution)/shard_map/panel_spread/pallas_call | solution.py:785
  266.5 0.0 copy-start.1
  266.5 2.0 copy-done.1
  268.5 0.0 copy-start.2
  268.5 0.8 copy-done.2
  269.3 0.0 all-to-all-done
  269.3 18.7 %trailing_front.1 = f32[4096,512]{1,0:T(8,128)} custom-call(s32[256]{0:T(256)} %reshape.290.place_ref, bf16[4096,512]{1,0:T(8,128)(2,1)} %copy-done.1, bf16[512,512]{1,0:T(8,128)(2,1)} %copy-done.2, bf16[4096,512]{1,0:T(8,128)(2,1)} %base_ref.3, bf16[256,128,128]{2,1,0:T(8,128)(2,1)} %bitcast.19.received_ref), custom_call_target="tpu_custom_call" | custom-call | tf_op jit(solution)/shard_map/trailing_front/pallas_call | solution.py:271
  288.0 0.0 copy-done.3
  (10 shorter events, 0.1 us)
Async XLA Ops:
  14.0 2.2 copy-start
  41.1 0.7 copy-start.4
  41.8 0.7 copy-start.5
  42.5 0.7 copy-start.6
  43.2 0.7 copy-start.7
  43.9 0.7 copy-start.8
  109.4 159.9 %all-to-all-start = ((bf16[128,2,128,128]{3,2,1,0:T(8,128)(2,1)}), bf16[128,2,128,128]{3,2,1,0:T(8,128)(2,1)}, u32[]{:S(2)}, u32[]{:S(2)}) async-start(bf16[128,2,128,128]{3,2,1,0:T(8,128)(2,1)} %bitcast.107), calls=%async_computation | async-start | bytes 16777216 | tf_op jit(solution)/shard_map/all_to_all | solution.py:857
  119.1 27.4 %copy-start.9 = (f32[128,512]{1,0:T(8,128)S(1)}, f32[128,512]{1,0:T(8,128)}, u32[]{:S(2)}) copy-start(f32[128,512]{1,0:T(8,128)} %front_rows.1) | copy-start | bytes 786436
  147.7 140.3 %copy-start.3 = (bf16[128,512]{1,0:T(8,128)(2,1)}, bf16[128,512]{1,0:T(8,128)(2,1)S(1)}, u32[]{:S(2)}) copy-start(bf16[128,512]{1,0:T(8,128)(2,1)S(1)} %fusion.panel_ref) | copy-start | bytes 393220
  266.5 2.0 copy-start.1
  268.5 0.8 copy-start.2

commit v5 on v4

--- a/solution.py
+++ b/solution.py
@@ -2,6 +2,7 @@
 
 import jax
 import jax.numpy as jnp
+import numpy as np
 from jax import lax
 from jax.experimental import pallas as pl
 from jax.experimental.pallas import tpu as pltpu
@@ -113,11 +114,10 @@
 
 
 def galerkin_tiles(slots, basis, link, diag, before_y, after_y, before_x, after_x):
-    k = jnp.arange(512)[:, None]
-    n = jnp.arange(256)[None, :]
-    stencil = (
-        (jnp.abs(k // 32 - 4 - n // 32) <= 1) & (jnp.abs(k % 32 - n % 32) <= 1)
-    ).astype(BF)
+    k = np.arange(512)[:, None]
+    n = np.arange(256)[None, :]
+    near = (abs(k // 32 - 4 - n // 32) <= 1) & (abs(k % 32 - n % 32) <= 1)
+    stencil = jnp.asarray(near.astype(np.float32), BF)
     cube = lambda t, s: (0, 0, 0)
     flat = lambda t, s: (0, 0)
     return pl.pallas_call(
@@ -225,33 +225,27 @@
     )(pivot_matrix)
 
 
-def final_kernel(place_ref, row_ref, col_ref, base_ref, received_ref, out_ref, sums):
+def final_kernel(
+    place_ref, order_ref, start_ref, row_ref, col_ref, base_ref, received_ref, out_ref, sums
+):
     step = pl.program_id(0)
     group = lax.axis_index("grp")
     member = lax.axis_index("sub")
-    row_start = group * 4096
+    first_row = group * 4096 + step * 512
     col_start = member * 512
-    live = (member > 0) & (row_start + 4095 >= col_start)
-
-    @pl.when(live & (step == 0))
+    live = (member > 0) & (first_row + 511 >= col_start)
+
+    @pl.when(live)
     def _():
         sums[...] = jnp.zeros_like(sums)
 
-        def add(slot, carry):
-            place = place_ref[slot]
-
-            @pl.when(place >= 0)
-            def _():
-                sums[place] = sums[place] + received_ref[slot].astype(F32)
-
-            return carry
-
-        lax.fori_loop(0, 256, add, 0)
-
-    first_row = row_start + step * 512
-
-    @pl.when(live & (first_row + 511 >= col_start))
-    def _():
+        def add(k, carry):
+            slot = order_ref[k]
+            place = place_ref[slot] - 16 * step
+            sums[place] = sums[place] + received_ref[slot].astype(F32)
+            return carry
+
+        lax.fori_loop(start_ref[step], start_ref[step + 1], add, 0)
         update = dotb(row_ref[...], col_ref[...], NT)
         rows = first_row + lax.broadcasted_iota(jnp.int32, (128, 128), 0)
         cols = col_start + lax.broadcasted_iota(jnp.int32, (128, 128), 1)
@@ -259,35 +253,45 @@
             for j in range(4):
                 r = slice(128 * i, 128 * i + 128)
                 c = slice(128 * j, 128 * j + 128)
-                value = base_ref[r, c].astype(F32) + sums[(step * 4 + i) * 4 + j] - update[r, c]
+                value = base_ref[r, c].astype(F32) + sums[i * 4 + j] - update[r, c]
                 out_ref[r, c] = jnp.where(rows + 128 * i >= cols + 128 * j, value, 0.0)
 
-    @pl.when(jnp.logical_not(live & (first_row + 511 >= col_start)))
+    @pl.when(jnp.logical_not(live))
     def _():
         out_ref[...] = jnp.zeros_like(out_ref)
 
 
 def trailing_front(place, panel_rows, panel_cols, base, received):
+    key = jnp.where(place < 0, 1 << 20, place)
+    ids = jnp.arange(256, dtype=jnp.int32)
+    before = (key[None, :] < key[:, None]) | (
+        (key[None, :] == key[:, None]) & (ids[None, :] < ids[:, None])
+    )
+    rank = jnp.sum(before.astype(jnp.int32), axis=1)
+    order = jnp.sum(jnp.where(rank[:, None] == ids[None, :], ids[:, None], 0), axis=0)
+    edges = 16 * jnp.arange(9, dtype=jnp.int32)
+    starts = jnp.sum((key[None, :] < edges[:, None]).astype(jnp.int32), axis=1)
+    once = pl.Buffered(1)
     return pl.pallas_call(
         final_kernel,
         out_shape=jax.ShapeDtypeStruct((4096, 512), F32),
         grid_spec=pltpu.PrefetchScalarGridSpec(
-            num_scalar_prefetch=1,
+            num_scalar_prefetch=3,
             grid=(8,),
             in_specs=[
-                pl.BlockSpec((512, 512), lambda t, s: (t, 0)),
-                pl.BlockSpec((512, 512), lambda t, s: (0, 0)),
-                pl.BlockSpec((512, 512), lambda t, s: (t, 0)),
-                pl.BlockSpec((256, 128, 128), lambda t, s: (0, 0, 0)),
+                pl.BlockSpec((512, 512), lambda t, *_: (t, 0)),
+                pl.BlockSpec((512, 512), lambda t, *_: (0, 0), pipeline_mode=once),
+                pl.BlockSpec((512, 512), lambda t, *_: (t, 0)),
+                pl.BlockSpec((256, 128, 128), lambda t, *_: (0, 0, 0), pipeline_mode=once),
             ],
-            out_specs=pl.BlockSpec((512, 512), lambda t, s: (t, 0)),
-            scratch_shapes=[pltpu.VMEM((128, 128, 128), F32)],
+            out_specs=pl.BlockSpec((512, 512), lambda t, *_: (t, 0)),
+            scratch_shapes=[pltpu.VMEM((16, 128, 128), F32)],
         ),
         compiler_params=pltpu.CompilerParams(
             dimension_semantics=("arbitrary",), vmem_limit_bytes=60 * 2**20
         ),
         name="trailing_front",
-    )(place, panel_rows, panel_cols, base, received)
+    )(place, order, starts, panel_rows, panel_cols, base, received)
 
 
 def at(group, member):
@@ -478,7 +482,7 @@
             dma((8,)), dma((8,)), dma((68,)), dma((32,)), dma((32,)), dma, dma((2,)),
         ],
         compiler_params=pltpu.CompilerParams(
-            collective_id=0, has_side_effects=True, vmem_limit_bytes=16 * 2**20
+            collective_id=0, has_side_effects=True, vmem_limit_bytes=60 * 2**20
         ),
         name="opening",
     )(high_x, low_x, high_y, low_y, base_front)
@@ -495,13 +499,27 @@
     takes = (member >= base) & (member < base + parts)
     barrier = pltpu.get_barrier_semaphore()
 
-    def greet(d, carry):
-        other = lax.rem(me + d, devices)
-        pl.semaphore_signal(barrier, 1, device_id=at(other // members, lax.rem(other, members)))
-        return carry
-
-    lax.fori_loop(1, devices, greet, 0)
-    pl.semaphore_wait(barrier, devices - 1)
+    @pl.when(takes)
+    def _():
+        def greet(d, carry):
+            other = lax.rem(me + d, devices)
+            pl.semaphore_signal(barrier, 1, device_id=at(other // members, lax.rem(other, members)))
+            return carry
+
+        lax.fori_loop(1, devices, greet, 0)
+
+    @pl.when(jnp.logical_not(takes))
+    def _():
+        for r in range(parts):
+            pl.semaphore_signal(barrier, 1, device_id=at(group, base + r))
+
+    @pl.when(jnp.logical_not(takes) & (member > 0))
+    def _():
+        pl.semaphore_signal(barrier, 1, device_id=at(group, 0))
+
+    pl.semaphore_wait(
+        barrier, groups * parts + jnp.where(takes | (member == 0), members - parts - 1, 0)
+    )
 
     def source(g, r):
         first = pl.ds(2 * members * g, 2)
@@ -548,15 +566,14 @@
         lax.fori_loop(EARLY, members, send, 0)
 
     def sum_copy(r, a):
-        rows = pl.ds(pl.multiple_of(16 * r, 16), 16)
         return pltpu.make_async_remote_copy(
-            sums.at[pl.ds(4 * a, 4)], added.at[:, rows], sum_send.at[a], sum_recv.at[r],
+            sums.at[pl.ds(4 * a, 4)], added.at[r], sum_send.at[a], sum_recv.at[r],
             device_id=at(group, a),
         )
 
     own_sum = pltpu.make_async_copy(
         sums.at[pl.ds(4 * member, 4)],
-        added.at[:, pl.ds(pl.multiple_of(16 * own_rank, 16), 16)],
+        added.at[own_rank],
         own_sem.at[1],
     )
 
@@ -592,18 +609,21 @@
     def _():
         own_sum.wait()
 
+    def summed(q):
+        return jnp.concatenate([added[r, q] for r in range(parts)], axis=0).astype(F32)
+
     @pl.when(member < EARLY)
     def _():
         for q in range(4):
             cols = slice(128 * q, 128 * q + 128)
-            front_ref[:, cols] = early_ref[:, cols].astype(F32) + added[q].astype(F32)
+            front_ref[:, cols] = early_ref[:, cols].astype(F32) + summed(q)
 
     @pl.when(member >= EARLY)
     def _():
         base_copy(member).wait_recv()
         for q in range(4):
             cols = slice(128 * q, 128 * q + 128)
-            front_ref[:, cols] = late[:, cols].astype(F32) + added[q].astype(F32)
+            front_ref[:, cols] = late[:, cols].astype(F32) + summed(q)
 
     def sent_strip(j, carry):
         g, r = target(j)
@@ -645,7 +665,7 @@
         scratch_shapes=[
             pltpu.VMEM((256, 16, 128), BF),
             pltpu.VMEM((128, 16, 128), BF),
-            pltpu.VMEM((4, 128, 128), BF),
+            pltpu.VMEM((8, 4, 16, 128), BF),
             pltpu.VMEM((128, 512), BF),
             dma((32,)), dma((128,)), dma((32,)), dma((8,)), dma((32,)), dma, dma((2,)),
         ],
@@ -664,7 +684,6 @@
     member = lax.axis_index("sub")
     chip = member // 2
     core = lax.rem(member, 2)
-    live = member // 8 <= group
     source_group = member // 8
     barrier = pltpu.get_barrier_semaphore()
 
@@ -697,6 +716,9 @@
             device_id=at(group, chip * 2 + 1 - core),
         )
 
+    def used(m, c):
+        return (c // 4 < group) | ((c // 4 == group) & (m >= 8 * lax.rem(c, 4)))
+
     def other(d):
         return lax.rem(chip + d, chips) * 2 + core
 
@@ -709,7 +731,7 @@
         )
 
     def spread(d, carry):
-        @pl.when(other(d) // 8 <= group)
+        @pl.when(used(member, other(d) // 2))
         def _():
             row_copy(member, d, other(d)).start()
 
@@ -731,28 +753,39 @@
 
     own_rows.start()
 
-    @pl.when(live)
+    @pl.when(used(member, chip))
     def _():
         fold_copy(member, panel_ref).start()
 
-        def fold(d, carry):
-            m = other(d)
+    def fold(d, carry):
+        m = other(d)
+
+        @pl.when(used(m, chip))
+        def _():
             row_copy(m, 0, member).wait_recv()
             fold_copy(m, rows_ref.at[block(m)]).start()
-            return carry
-
-        lax.fori_loop(1, chips, fold, 0)
-
-        def folded(d, carry):
-            m = lax.rem(chip + d, chips) * 2
+
+        return carry
+
+    lax.fori_loop(1, chips, fold, 0)
+
+    def folded(d, carry):
+        m = lax.rem(chip + d, chips) * 2
+
+        @pl.when(used(m + 1 - core, chip))
+        def _():
             fold_copy(m + 1 - core, panel_ref).wait_recv()
+
+        @pl.when(used(m + core, chip))
+        def _():
             fold_copy(m + core, panel_ref).wait_send()
-            return carry
-
-        lax.fori_loop(0, chips, folded, 0)
+
+        return carry
+
+    lax.fori_loop(0, chips, folded, 0)
 
     def sent(d, carry):
-        @pl.when(other(d) // 8 <= group)
+        @pl.when(used(member, other(d) // 2))
         def _():
             row_copy(member, d, other(d)).wait_send()
 
@@ -791,7 +824,7 @@
             dma((16,)), dma((16,)), dma((16,)), dma((16,)), dma((4,)), dma((4,)), dma((2,)),
         ],
         compiler_params=pltpu.CompilerParams(
-            collective_id=1, has_side_effects=True, vmem_limit_bytes=16 * 2**20
+            collective_id=1, has_side_effects=True, vmem_limit_bytes=60 * 2**20
         ),
         name="panel_spread",
     )(panel)

time: 289 us -> 278 us (0.962)
  local copies, waits for them, and re-layouts: 20.3 us -> 11.3 us
  Pallas kernels: 252 us -> 246 us
    unnamed x21 -> x7, local copies, waits for them, and re-layouts: 9.33 us -> 0.93 us
    pallas_call x1, Pallas kernels: 18.7 us -> 15.3 us  [trailing_front(): pl.pallas_call(final_kernel, out_shape=jax.ShapeDtypeStruct((4096, 512),...]
    pallas_call x1, Pallas kernels: 39.2 us -> 36.2 us  [front_rows_of(): pl.pallas_call(front_kernel, out_shape=jax.ShapeDtypeStruct((128, 512), F...]
  transfers between devices with their start and end apart: 1 -> 1, of which waited for: 0 -> 0; matrix products, arithmetic and copies ran while one was open for 1% -> 2% of each run, Pallas kernels for 50% -> 51%
where the time goes in v5:
time: 278 us; the launch traced here: 276 us
  Pallas kernels  246 us (88%)
  local copies, waits for them, and re-layouts  11.3 us (4%)
  starting transfers between devices  9.86 us (4%)
  other arithmetic  5.91 us (2%)
    pallas_call x1, Pallas kernels, panel_spread(): pl.pallas_call(panel_kernel, out_shape=[jax.ShapeDtypeStruct((4096, 512),...  116 us
    pallas_call x1, Pallas kernels, front_rows_of(): pl.pallas_call(front_kernel, out_shape=jax.ShapeDtypeStruct((128, 512), F...  36.2 us
    pallas_call x1, Pallas kernels, opening(): pl.pallas_call(opening_kernel, out_shape=[jax.ShapeDtypeStruct((1024, 128...  27.5 us
    pallas_call x1, Pallas kernels, galerkin_tiles(): pl.pallas_call(tile_kernel, out_shape=jax.ShapeDtypeStruct((256, 128, 128...  25.6 us
    pallas_call x1, Pallas kernels, pivot_factor(): pl.pallas_call(factor_kernel, out_shape=[jax.ShapeDtypeStruct((size, size...  25 us
    pallas_call x1, Pallas kernels, trailing_front(): pl.pallas_call(final_kernel, out_shape=jax.ShapeDtypeStruct((4096, 512),...  15.3 us
    all_to_all x1, starting transfers between devices, per_device(): lax.all_to_all(outgoing.reshape(devices, 2, 128, 128), ('grp', 'sub'), sp...  9.86 us
  transfers between devices with their start and end apart: 1, of which 0 were waited for; matrix products, arithmetic and copies ran while one was open for 2% of the time, Pallas kernels for 51%

profile of v5, /device:TPU:121, one launch (start us, length us, event | category | flops | bytes accessed | tf_op | source)
XLA Modules:
  0.0 276.0 jit_solution(11081746898982561984)
XLA Ops:
  0.6 1.1 slice_reduce_fusion
  1.7 0.7 fusion.29
  2.4 0.9 copy.29
  3.4 0.2 select_reduce_fusion.6
  3.6 0.2 select_reduce_fusion.5
  3.8 2.0 reshape.203.link_ref
  5.8 1.1 fusion.27
  6.8 1.1 fusion.28
  7.9 0.1 mul.105
  8.0 0.1 mul.102
  8.1 0.1 mul.99
  8.1 0.1 mul.96
  8.2 1.9 reshape.204.diag_ref
  10.2 0.2 convert_reduce_fusion.1
  10.3 0.5 multiply_add_fusion.slot_ref
  10.8 0.1 copy.19
  11.0 0.1 lt.127
  11.1 0.1 copy.20
  11.2 0.1 mul.112
  11.4 0.1 add_select_fusion
  11.5 0.7 select_n.132.key_ref
  12.2 1.2 fusion.1
  13.4 1.1 fusion.3
  14.5 27.5 %opening.1 = (bf16[1024,128]{1,0:T(8,128)(2,1)}, bf16[1024,128]{1,0:T(8,128)(2,1)}, bf16[1088,128]{1,0:T(8,128)(2,1)}, bf16[1088,128]{1,0:T(8,128)(2,1)}, bf16[5...) custom-call(bf16[1024,128]{1,0:T(8,128)(2,1)} %get-tuple-element.55.high_x, bf16[1024,128]{1,0:T(8,128)(2,1)} %get-tuple-element.54.low_x, ...), custom_call_target="tpu_custom_call" | custom-call | tf_op jit(solution)/shard_map/opening/pallas_call | solution.py:469
  42.1 25.6 %galerkin_tiles.1.tiles_ref = bf16[256,128,128]{2,1,0:T(8,128)(2,1)} custom-call(s32[128]{0:T(128)} %multiply_add_fusion.slot_ref, bf16[32,1024,128]{2,1,0:T(8,128)(2,1)} %bitcast.106, f32[32,1,1024]{2,1,0:T(1,128)} %reshape.203.link_ref, f32[32,1,1024]{2,1,0:T(1,128)} %reshape.204.diag_ref, bf16[34,32,128]{2,1,0:T(8,128)(2,1)} %bitcast.110, ...), custom_call_target="tpu_custom_call" | custom-call | tf_op jit(solution)/shard_map/galerkin_tiles/pallas_call | solution.py:123
  67.7 36.2 %front_rows.1 = f32[128,512]{1,0:T(8,128)} custom-call(s32[1,4096]{1,0:T(1,128)} %select_n.132.key_ref, bf16[256,128,128]{2,1,0:T(8,128)(2,1)} %galerkin_tiles.1.tiles_ref, bf16[4096,512]{1,0:T(8,128)(2,1)} %base_ref.3, bf16[128,512]{1,0:T(8,128)(2,1)} %get-tuple-element.22.early_ref), custom_call_target="tpu_custom_call" | custom-call | tf_op jit(solution)/shard_map/front_rows/pallas_call | solution.py:660
  103.9 0.0 copy-start.1
  103.9 9.9 %all-to-all-start = ((bf16[128,2,128,128]{3,2,1,0:T(8,128)(2,1)}), bf16[128,2,128,128]{3,2,1,0:T(8,128)(2,1)}, u32[]{:S(2)}, u32[]{:S(2)}) async-start(bf16[128,2,128,128]{3,2,1,0:T(8,128)(2,1)} %bitcast.105), calls=%async_computation | async-start | bytes 16777216 | tf_op jit(solution)/shard_map/all_to_all | solution.py:890
  113.8 0.0 copy-start
  113.8 0.1 select_reduce_fusion.3
  113.9 0.2 select_reduce_fusion.2
  114.1 0.1 copy.21
  114.2 0.1 reshape.207.place_ref
  114.4 0.0 copy-done.1
  114.4 0.0 copy-start.2
  114.4 0.2 copy.22
  114.6 0.2 copy.24
  114.9 0.3 abs_reduce_fusion
  115.2 0.3 copy.25
  115.5 0.1 select_add_fusion.pivot_ref
  115.7 25.0 %pivot_factor.1 = (f32[512,512]{1,0:T(8,128)S(1)}, f32[512,512]{1,0:T(8,128)S(1)}) custom-call(f32[512,512]{1,0:T(8,128)S(1)} %select_add_fusion.pivot_ref), custom_call_target="tpu_custom_call" | custom-call | tf_op jit(solution)/shard_map/pivot_factor/pallas_call | solution.py:217
  140.7 0.0 copy-done
  140.7 1.8 fusion.panel_ref
  142.5 116.5 %panel_spread.1 = (bf16[4096,512]{1,0:T(8,128)(2,1)}, bf16[512,512]{1,0:T(8,128)(2,1)}) custom-call(bf16[128,512]{1,0:T(8,128)(2,1)} %fusion.panel_ref), custom_call_target="tpu_custom_call" | custom-call | tf_op jit(solution)/shard_map/panel_spread/pallas_call | solution.py:818
  259.0 0.7 convert_reduce_fusion.2.start_ref
  259.7 0.2 convert_reduce_fusion
  259.9 0.7 select_reduce_fusion.order_ref
  260.6 0.0 all-to-all-done
  260.6 0.0 copy-done.2
  260.7 15.3 %trailing_front.1 = f32[4096,512]{1,0:T(8,128)} custom-call(s32[256]{0:T(256)} %copy-done.2, s32[256]{0:T(256)} %select_reduce_fusion.order_ref, s32[9]{0:T(128)} %convert_reduce_fusion.2.start_ref, bf16[4096,512]{1,0:T(8,128)(2,1)} %get-tuple-element.29.row_ref, bf16[512,512]{1,0:T(8,128)(2,1)} %get-tuple-element.30.col_ref, bf16[4096,512]{1,0:T(8,128)(2,1)} %base_ref.3, ...), custom_call_target="tpu_custom_call" | custom-call | tf_op jit(solution)/shard_map/trailing_front/pallas_call | solution.py:275
  (10 shorter events, 0.1 us)
Async XLA Ops:
  103.9 10.5 %copy-start.1 = (bf16[512,512]{1,0:T(8,128)(2,1)S(1)}, bf16[512,512]{1,0:T(8,128)(2,1)}, u32[]{:S(2)}) copy-start(bf16[512,512]{1,0:T(8,128)(2,1)} %get-tuple-element.25) | copy-start | bytes 1572868
  103.9 156.7 %all-to-all-start = ((bf16[128,2,128,128]{3,2,1,0:T(8,128)(2,1)}), bf16[128,2,128,128]{3,2,1,0:T(8,128)(2,1)}, u32[]{:S(2)}, u32[]{:S(2)}) async-start(bf16[128,2,128,128]{3,2,1,0:T(8,128)(2,1)} %bitcast.105), calls=%async_computation | async-start | bytes 16777216 | tf_op jit(solution)/shard_map/all_to_all | solution.py:890
  113.8 26.9 %copy-start = (f32[128,512]{1,0:T(8,128)S(1)}, f32[128,512]{1,0:T(8,128)}, u32[]{:S(2)}) copy-start(f32[128,512]{1,0:T(8,128)} %front_rows.1) | copy-start | bytes 786436
  114.4 146.2 %copy-start.2 = (s32[256]{0:T(256)}, s32[256]{0:T(256)S(1)}, u32[]{:S(2)}) copy-start(s32[256]{0:T(256)S(1)} %reshape.207.place_ref) | copy-start | bytes 3076

commit v6 on v5

--- a/solution.py
+++ b/solution.py
@@ -677,12 +677,14 @@
 
 
 def panel_kernel(
-    panel_ref, rows_ref, cols_ref, send, recv, fold_send, fold_recv, col_send, col_recv, own_sem
+    panel_ref, rows_ref, cols_ref,
+    send, recv, fold_send, fold_recv, col_send, col_recv, own_sem,
 ):
-    groups, members, chips = 4, 32, 16
+    groups, members = 4, 32
     group = lax.axis_index("grp")
     member = lax.axis_index("sub")
-    chip = member // 2
+    x = member // 8
+    z = lax.rem(member // 2, 4)
     core = lax.rem(member, 2)
     source_group = member // 8
     barrier = pltpu.get_barrier_semaphore()
@@ -705,22 +707,55 @@
     def block(m):
         return pl.ds(pl.multiple_of(128 * m, 128), 128)
 
-    def row_copy(m, k, s):
+    def half_rows(m, half):
+        return pl.ds(pl.multiple_of(128 * m + 64 * half, 64), 64)
+
+    def wrap(v):
+        return lax.rem(v + 4, 4)
+
+    def where(bx, bz):
+        return bx * 8 + bz * 2 + core
+
+    pending = []
+
+    def pass_on(half, bx, bz, own, dx, dz, condition):
+        k = len(pending)
+        m = where(bx, bz)
+        source = panel_ref.at[pl.ds(64 * half, 64)] if own else rows_ref.at[half_rows(m, half)]
+        copy = pltpu.make_async_remote_copy(
+            source, rows_ref.at[half_rows(m, half)], send.at[k], recv.at[half, bx * 4 + bz],
+            device_id=at(group, where(wrap(x + dx), wrap(z + dz))),
+        )
+        pending.append((copy, condition))
+        if condition is None:
+            copy.start()
+        else:
+            pl.when(condition)(copy.start)
+
+    def fold_copy(half, bx, bz, side, source=None):
+        m = bx * 8 + bz * 2 + side
+        if source is None:
+            source = rows_ref.at[half_rows(m, half)]
         return pltpu.make_async_remote_copy(
-            panel_ref, rows_ref.at[block(m)], send.at[k], recv.at[m // 2], device_id=at(group, s)
+            source, rows_ref.at[half_rows(m, half)],
+            fold_send.at[half, bx * 4 + bz], fold_recv.at[half, bx * 4 + bz],
+            device_id=at(group, x * 8 + z * 2 + 1 - core),
         )
 
-    def fold_copy(m, source):
-        return pltpu.make_async_remote_copy(
-            source, rows_ref.at[block(m)], fold_send.at[m // 2], fold_recv.at[m // 2],
-            device_id=at(group, chip * 2 + 1 - core),
-        )
-
-    def used(m, c):
-        return (c // 4 < group) | ((c // 4 == group) & (m >= 8 * lax.rem(c, 4)))
-
-    def other(d):
-        return lax.rem(chip + d, chips) * 2 + core
+    def arrived(half, bx, bz):
+        pltpu.make_async_remote_copy(
+            panel_ref.at[pl.ds(0, 64)], rows_ref.at[half_rows(where(bx, bz), half)],
+            send.at[0], recv.at[half, bx * 4 + bz], device_id=at(group, member),
+        ).wait_recv()
+        fold_copy(half, bx, bz, core).start()
+
+    steps = (1, -1)
+    for d in steps:
+        pass_on(0, x, z, True, 0, d, None)
+        pass_on(1, x, z, True, d, 0, None)
+    for d in steps:
+        pass_on(0, x, z, True, d, 0, None)
+        pass_on(1, x, z, True, 0, d, None)
 
     target = group * 8 + member // 4
     quarter = lax.rem(member, 4)
@@ -730,15 +765,6 @@
             panel_ref, cols_ref.at[block(q)], col_send.at[g], col_recv.at[q], device_id=at(g, s)
         )
 
-    def spread(d, carry):
-        @pl.when(used(member, other(d) // 2))
-        def _():
-            row_copy(member, d, other(d)).start()
-
-        return carry
-
-    lax.fori_loop(1, chips, spread, 0)
-
     for g in range(groups):
         @pl.when((g >= group) & jnp.logical_not((g == group) & (target == member)))
         def _():
@@ -752,46 +778,51 @@
         own_cols.start()
 
     own_rows.start()
-
-    @pl.when(used(member, chip))
-    def _():
-        fold_copy(member, panel_ref).start()
-
-    def fold(d, carry):
-        m = other(d)
-
-        @pl.when(used(m, chip))
-        def _():
-            row_copy(m, 0, member).wait_recv()
-            fold_copy(m, rows_ref.at[block(m)]).start()
-
+    for half in range(2):
+        fold_copy(half, x, z, core, panel_ref.at[pl.ds(64 * half, 64)]).start()
+
+    even = lambda v: lax.rem(v, 2) == 0
+    odd = lambda v: lax.rem(v, 2) == 1
+    for d in steps:
+        bz = wrap(z - d)
+        arrived(0, x, bz)
+        pass_on(0, x, bz, False, 0, d, even(bz) if d == 1 else odd(bz))
+        bx = wrap(x - d)
+        arrived(1, bx, z)
+        pass_on(1, bx, z, False, d, 0, even(bx) if d == 1 else odd(bx))
+        for e in steps:
+            pass_on(0, x, bz, False, e, 0, None)
+            pass_on(1, bx, z, False, 0, e, None)
+    far_z, far_x = wrap(z + 2), wrap(x + 2)
+    arrived(0, x, far_z)
+    arrived(1, far_x, z)
+    for e in steps:
+        pass_on(0, x, far_z, False, e, 0, None)
+        pass_on(1, far_x, z, False, 0, e, None)
+    for o in (0, 1, 3, 2):
+        for d in steps:
+            bx, bz = wrap(x - d), wrap(z + o)
+            arrived(0, bx, bz)
+            pass_on(0, bx, bz, False, d, 0, even(bz) if d == 1 else odd(bz))
+            bx, bz = wrap(x + o), wrap(z - d)
+            arrived(1, bx, bz)
+            pass_on(1, bx, bz, False, 0, d, even(bx) if d == 1 else odd(bx))
+    for o in (0, 1, 3, 2):
+        arrived(0, far_x, wrap(z + o))
+        arrived(1, wrap(x + o), far_z)
+
+    def folded(n, carry):
+        for half in range(2):
+            fold_copy(half, n // 4, lax.rem(n, 4), 1 - core).wait_recv()
+            fold_copy(half, n // 4, lax.rem(n, 4), core).wait_send()
         return carry
 
-    lax.fori_loop(1, chips, fold, 0)
-
-    def folded(d, carry):
-        m = lax.rem(chip + d, chips) * 2
-
-        @pl.when(used(m + 1 - core, chip))
-        def _():
-            fold_copy(m + 1 - core, panel_ref).wait_recv()
-
-        @pl.when(used(m + core, chip))
-        def _():
-            fold_copy(m + core, panel_ref).wait_send()
-
-        return carry
-
-    lax.fori_loop(0, chips, folded, 0)
-
-    def sent(d, carry):
-        @pl.when(used(member, other(d) // 2))
-        def _():
-            row_copy(member, d, other(d)).wait_send()
-
-        return carry
-
-    lax.fori_loop(1, chips, sent, 0)
+    lax.fori_loop(0, 16, folded, 0)
+    for copy, condition in pending:
+        if condition is None:
+            copy.wait_send()
+        else:
+            pl.when(condition)(copy.wait_send)
     for g in range(groups):
         @pl.when((g >= group) & jnp.logical_not((g == group) & (target == member)))
         def _():
@@ -821,7 +852,7 @@
         in_specs=[pl.BlockSpec(memory_space=pltpu.VMEM)],
         out_specs=[anywhere, anywhere],
         scratch_shapes=[
-            dma((16,)), dma((16,)), dma((16,)), dma((16,)), dma((4,)), dma((4,)), dma((2,)),
+            dma((40,)), dma((2, 16)), dma((2, 16)), dma((2, 16)), dma((4,)), dma((4,)), dma((2,)),
         ],
         compiler_params=pltpu.CompilerParams(
             collective_id=1, has_side_effects=True, vmem_limit_bytes=60 * 2**20

time: 278 us -> 269 us (0.968)
  the two profiles are of different devices: /device:TPU:121 before, /device:TPU:1 now
where the time goes in v6:
time: 269 us; the launch traced here: 268 us
  Pallas kernels  242 us (90%)
  local copies, waits for them, and re-layouts  11.3 us (4%)
  starting transfers between devices  6.48 us (2%)
  other arithmetic  5.91 us (2%)
    pallas_call x1, Pallas kernels, panel_spread(): pl.pallas_call(panel_kernel, out_shape=[jax.ShapeDtypeStruct((4096, 512),...  108 us
    pallas_call x1, Pallas kernels, front_rows_of(): pl.pallas_call(front_kernel, out_shape=jax.ShapeDtypeStruct((128, 512), F...  40.1 us
    pallas_call x1, Pallas kernels, opening(): pl.pallas_call(opening_kernel, out_shape=[jax.ShapeDtypeStruct((1024, 128...  28.5 us
    pallas_call x1, Pallas kernels, galerkin_tiles(): pl.pallas_call(tile_kernel, out_shape=jax.ShapeDtypeStruct((256, 128, 128...  25.7 us
    pallas_call x1, Pallas kernels, pivot_factor(): pl.pallas_call(factor_kernel, out_shape=[jax.ShapeDtypeStruct((size, size...  25 us
    pallas_call x1, Pallas kernels, trailing_front(): pl.pallas_call(final_kernel, out_shape=jax.ShapeDtypeStruct((4096, 512),...  14.9 us
    all_to_all x1, starting transfers between devices, per_device(): lax.all_to_all(outgoing.reshape(devices, 2, 128, 128), ('grp', 'sub'), sp...  6.48 us
  transfers between devices with their start and end apart: 1, of which 0 were waited for; matrix products, arithmetic and copies ran while one was open for 2% of the time, Pallas kernels for 49%

profile of v6, /device:TPU:1, one launch (start us, length us, event | category | flops | bytes accessed | tf_op | source)
XLA Modules:
  0.0 268.1 jit_solution(7384975472658649892)
XLA Ops:
  0.6 1.1 slice_reduce_fusion
  1.7 0.7 fusion.29
  2.4 0.9 copy.29
  3.4 0.2 select_reduce_fusion.6
  3.6 0.2 select_reduce_fusion.5
  3.8 2.0 reshape.203.link_ref
  5.8 1.1 fusion.27
  6.8 1.1 fusion.28
  7.9 0.1 mul.105
  8.0 0.1 mul.102
  8.1 0.1 mul.99
  8.1 0.1 mul.96
  8.2 1.9 reshape.204.diag_ref
  10.2 0.2 convert_reduce_fusion.1
  10.3 0.5 multiply_add_fusion.slot_ref
  10.8 0.1 copy.19
  11.0 0.1 lt.127
  11.1 0.1 copy.20
  11.2 0.1 mul.112
  11.4 0.1 add_select_fusion
  11.5 0.7 select_n.132.key_ref
  12.2 1.2 fusion.1
  13.4 1.1 fusion.3
  14.5 28.5 %opening.1 = (bf16[1024,128]{1,0:T(8,128)(2,1)}, bf16[1024,128]{1,0:T(8,128)(2,1)}, bf16[1088,128]{1,0:T(8,128)(2,1)}, bf16[1088,128]{1,0:T(8,128)(2,1)}, bf16[5...) custom-call(bf16[1024,128]{1,0:T(8,128)(2,1)} %get-tuple-element.55.high_x, bf16[1024,128]{1,0:T(8,128)(2,1)} %get-tuple-element.54.low_x, ...), custom_call_target="tpu_custom_call" | custom-call | tf_op jit(solution)/shard_map/opening/pallas_call | solution.py:469
  43.0 25.7 %galerkin_tiles.1.tiles_ref = bf16[256,128,128]{2,1,0:T(8,128)(2,1)} custom-call(s32[128]{0:T(128)} %multiply_add_fusion.slot_ref, bf16[32,1024,128]{2,1,0:T(8,128)(2,1)} %bitcast.106, f32[32,1,1024]{2,1,0:T(1,128)} %reshape.203.link_ref, f32[32,1,1024]{2,1,0:T(1,128)} %reshape.204.diag_ref, bf16[34,32,128]{2,1,0:T(8,128)(2,1)} %bitcast.110, ...), custom_call_target="tpu_custom_call" | custom-call | tf_op jit(solution)/shard_map/galerkin_tiles/pallas_call | solution.py:123
  68.7 40.1 %front_rows.1 = f32[128,512]{1,0:T(8,128)} custom-call(s32[1,4096]{1,0:T(1,128)} %select_n.132.key_ref, bf16[256,128,128]{2,1,0:T(8,128)(2,1)} %galerkin_tiles.1.tiles_ref, bf16[4096,512]{1,0:T(8,128)(2,1)} %base_ref.3, bf16[128,512]{1,0:T(8,128)(2,1)} %get-tuple-element.22.early_ref), custom_call_target="tpu_custom_call" | custom-call | tf_op jit(solution)/shard_map/front_rows/pallas_call | solution.py:660
  108.8 0.0 copy-start.1
  108.8 6.5 %all-to-all-start = ((bf16[128,2,128,128]{3,2,1,0:T(8,128)(2,1)}), bf16[128,2,128,128]{3,2,1,0:T(8,128)(2,1)}, u32[]{:S(2)}, u32[]{:S(2)}) async-start(bf16[128,2,128,128]{3,2,1,0:T(8,128)(2,1)} %bitcast.105), calls=%async_computation | async-start | bytes 16777216 | tf_op jit(solution)/shard_map/all_to_all | solution.py:921
  115.3 0.0 copy-start
  115.3 0.1 select_reduce_fusion.3
  115.4 0.2 select_reduce_fusion.2
  115.6 0.1 copy.21
  115.7 0.1 reshape.207.place_ref
  115.9 0.0 copy-done.1
  115.9 0.0 copy-start.2
  115.9 0.2 copy.22
  116.1 0.2 copy.24
  116.3 0.3 abs_reduce_fusion
  116.6 0.3 copy.25
  117.0 0.1 select_add_fusion.pivot_ref
  117.1 25.0 %pivot_factor.1 = (f32[512,512]{1,0:T(8,128)S(1)}, f32[512,512]{1,0:T(8,128)S(1)}) custom-call(f32[512,512]{1,0:T(8,128)S(1)} %select_add_fusion.pivot_ref), custom_call_target="tpu_custom_call" | custom-call | tf_op jit(solution)/shard_map/pivot_factor/pallas_call | solution.py:217
  142.1 0.0 copy-done
  142.2 1.8 fusion.panel_ref
  144.0 107.5 %panel_spread.1 = (bf16[4096,512]{1,0:T(8,128)(2,1)}, bf16[512,512]{1,0:T(8,128)(2,1)}) custom-call(bf16[128,512]{1,0:T(8,128)(2,1)} %fusion.panel_ref), custom_call_target="tpu_custom_call" | custom-call | tf_op jit(solution)/shard_map/panel_spread/pallas_call | solution.py:849
  251.6 0.7 convert_reduce_fusion.2.start_ref
  252.3 0.2 convert_reduce_fusion
  252.4 0.7 select_reduce_fusion.order_ref
  253.2 0.0 all-to-all-done
  253.2 0.0 copy-done.2
  253.2 14.9 %trailing_front.1 = f32[4096,512]{1,0:T(8,128)} custom-call(s32[256]{0:T(256)} %copy-done.2, s32[256]{0:T(256)} %select_reduce_fusion.order_ref, s32[9]{0:T(128)} %convert_reduce_fusion.2.start_ref, bf16[4096,512]{1,0:T(8,128)(2,1)} %get-tuple-element.29.row_ref, bf16[512,512]{1,0:T(8,128)(2,1)} %get-tuple-element.30.col_ref, bf16[4096,512]{1,0:T(8,128)(2,1)} %base_ref.3, ...), custom_call_target="tpu_custom_call" | custom-call | tf_op jit(solution)/shard_map/trailing_front/pallas_call | solution.py:275
  (10 shorter events, 0.1 us)
Async XLA Ops:
  108.8 7.1 %copy-start.1 = (bf16[512,512]{1,0:T(8,128)(2,1)S(1)}, bf16[512,512]{1,0:T(8,128)(2,1)}, u32[]{:S(2)}) copy-start(bf16[512,512]{1,0:T(8,128)(2,1)} %get-tuple-element.25) | copy-start | bytes 1572868
  108.8 144.4 %all-to-all-start = ((bf16[128,2,128,128]{3,2,1,0:T(8,128)(2,1)}), bf16[128,2,128,128]{3,2,1,0:T(8,128)(2,1)}, u32[]{:S(2)}, u32[]{:S(2)}) async-start(bf16[128,2,128,128]{3,2,1,0:T(8,128)(2,1)} %bitcast.105), calls=%async_computation | async-start | bytes 16777216 | tf_op jit(solution)/shard_map/all_to_all | solution.py:921
  115.3 26.9 %copy-start = (f32[128,512]{1,0:T(8,128)S(1)}, f32[128,512]{1,0:T(8,128)}, u32[]{:S(2)}) copy-start(f32[128,512]{1,0:T(8,128)} %front_rows.1) | copy-start | bytes 786436
  115.9 137.3 %copy-start.2 = (s32[256]{0:T(256)}, s32[256]{0:T(256)S(1)}, u32[]{:S(2)}) copy-start(s32[256]{0:T(256)S(1)} %reshape.207.place_ref) | copy-start | bytes 3076

commit v7 on v6

--- a/solution.py
+++ b/solution.py
@@ -489,7 +489,7 @@
 
 
 def front_kernel(
-    key_ref, tiles_ref, base_front_ref, early_ref, front_ref, strips, sums, added, late,
+    key_ref, tiles_ref, base_front_ref, early_ref, front_ref, strips, total, sums, added, late,
     strip_send, strip_recv, sum_send, sum_recv, base_send, base_recv, own_sem,
 ):
     groups, members, devices, parts, base = 4, 32, 128, 8, 8
@@ -581,17 +581,32 @@
     def _():
         own_strip.start()
 
-        def arrive(d, carry):
-            strip_copy(lax.rem(me + d, devices), group, own_rank, 0).wait_recv()
-            return carry
-
-        lax.fori_loop(1, devices, arrive, 0)
-        own_strip.wait()
-        rows = strips[...].reshape(4096, 128)
+        ids = lax.broadcasted_iota(jnp.int32, (2048, 512), 0)
         for n in range(8):
-            ids = 256 * n + lax.broadcasted_iota(jnp.int32, (256, 4096), 0)
-            pick = jnp.where(key_ref[...] == ids, 1.0, 0.0).astype(BF)
-            sums[16 * n:16 * n + 16] = dotb(pick, rows, NN).astype(BF).reshape(16, 16, 128)
+            def arrive(k, carry):
+                sender = 16 * n + k
+
+                @pl.when(sender != me)
+                def _():
+                    strip_copy(sender, group, own_rank, 0).wait_recv()
+
+                return carry
+
+            lax.fori_loop(0, 16, arrive, 0)
+
+            @pl.when(me // 16 == n)
+            def _():
+                own_strip.wait()
+
+            rows = strips[32 * n:32 * n + 32].reshape(512, 128)
+            pick = jnp.where(key_ref[:, 512 * n:512 * n + 512] == ids, 1.0, 0.0).astype(BF)
+            part = dotb(pick, rows, NN)
+            if n == 0:
+                total[...] = part
+            elif n < 7:
+                total[...] += part
+            else:
+                sums[...] = (total[...] + part).astype(BF).reshape(128, 16, 128)
 
         def send(d, carry):
             sum_copy(own_rank, lax.rem(member + d, members)).start()
@@ -664,6 +679,7 @@
         out_specs=vmem,
         scratch_shapes=[
             pltpu.VMEM((256, 16, 128), BF),
+            pltpu.VMEM((2048, 128), F32),
             pltpu.VMEM((128, 16, 128), BF),
             pltpu.VMEM((8, 4, 16, 128), BF),
             pltpu.VMEM((128, 512), BF),

time: 269 us -> 272 us (1.011)
  no operation moved by 1% of the time
where the time goes in v7:
time: 272 us; the launch traced here: 271 us
  Pallas kernels  243 us (89%)
  local copies, waits for them, and re-layouts  11.3 us (4%)
  starting transfers between devices  8.29 us (3%)
  other arithmetic  5.91 us (2%)
    pallas_call x1, Pallas kernels, panel_spread(): pl.pallas_call(panel_kernel, out_shape=[jax.ShapeDtypeStruct((4096, 512),...  108 us
    pallas_call x1, Pallas kernels, front_rows_of(): pl.pallas_call(front_kernel, out_shape=jax.ShapeDtypeStruct((128, 512), F...  41.7 us
    pallas_call x1, Pallas kernels, opening(): pl.pallas_call(opening_kernel, out_shape=[jax.ShapeDtypeStruct((1024, 128...  28.5 us
    pallas_call x1, Pallas kernels, galerkin_tiles(): pl.pallas_call(tile_kernel, out_shape=jax.ShapeDtypeStruct((256, 128, 128...  25.7 us
    pallas_call x1, Pallas kernels, pivot_factor(): pl.pallas_call(factor_kernel, out_shape=[jax.ShapeDtypeStruct((size, size...  25 us
    pallas_call x1, Pallas kernels, trailing_front(): pl.pallas_call(final_kernel, out_shape=jax.ShapeDtypeStruct((4096, 512),...  14.7 us
    all_to_all x1, starting transfers between devices, per_device(): lax.all_to_all(outgoing.reshape(devices, 2, 128, 128), ('grp', 'sub'), sp...  8.29 us
  transfers between devices with their start and end apart: 1, of which 0 were waited for; matrix products, arithmetic and copies ran while one was open for 2% of the time, Pallas kernels for 49%

profile of v7, /device:TPU:1, one launch (start us, length us, event | category | flops | bytes accessed | tf_op | source)
XLA Modules:
  0.0 271.3 jit_solution(4615516908999493254)
XLA Ops:
  0.6 1.1 slice_reduce_fusion
  1.7 0.7 fusion.29
  2.4 0.9 copy.29
  3.4 0.2 select_reduce_fusion.6
  3.6 0.2 select_reduce_fusion.5
  3.8 2.0 reshape.203.link_ref
  5.8 1.1 fusion.27
  6.8 1.1 fusion.28
  7.9 0.1 mul.105
  8.0 0.1 mul.102
  8.1 0.1 mul.99
  8.1 0.1 mul.96
  8.2 1.9 reshape.204.diag_ref
  10.2 0.2 convert_reduce_fusion.1
  10.3 0.5 multiply_add_fusion.slot_ref
  10.8 0.1 copy.19
  11.0 0.1 lt.127
  11.1 0.1 copy.20
  11.2 0.1 mul.112
  11.4 0.1 add_select_fusion
  11.5 0.7 select_n.132.key_ref
  12.2 1.2 fusion.1
  13.4 1.1 fusion.3
  14.5 28.5 %opening.1 = (bf16[1024,128]{1,0:T(8,128)(2,1)}, bf16[1024,128]{1,0:T(8,128)(2,1)}, bf16[1088,128]{1,0:T(8,128)(2,1)}, bf16[1088,128]{1,0:T(8,128)(2,1)}, bf16[5...) custom-call(bf16[1024,128]{1,0:T(8,128)(2,1)} %get-tuple-element.55.high_x, bf16[1024,128]{1,0:T(8,128)(2,1)} %get-tuple-element.54.low_x, ...), custom_call_target="tpu_custom_call" | custom-call | tf_op jit(solution)/shard_map/opening/pallas_call | solution.py:469
  43.0 25.7 %galerkin_tiles.1.tiles_ref = bf16[256,128,128]{2,1,0:T(8,128)(2,1)} custom-call(s32[128]{0:T(128)} %multiply_add_fusion.slot_ref, bf16[32,1024,128]{2,1,0:T(8,128)(2,1)} %bitcast.106, f32[32,1,1024]{2,1,0:T(1,128)} %reshape.203.link_ref, f32[32,1,1024]{2,1,0:T(1,128)} %reshape.204.diag_ref, bf16[34,32,128]{2,1,0:T(8,128)(2,1)} %bitcast.110, ...), custom_call_target="tpu_custom_call" | custom-call | tf_op jit(solution)/shard_map/galerkin_tiles/pallas_call | solution.py:123
  68.7 41.7 %front_rows.1 = f32[128,512]{1,0:T(8,128)} custom-call(s32[1,4096]{1,0:T(1,128)} %select_n.132.key_ref, bf16[256,128,128]{2,1,0:T(8,128)(2,1)} %galerkin_tiles.1.tiles_ref, bf16[4096,512]{1,0:T(8,128)(2,1)} %base_ref.3, bf16[128,512]{1,0:T(8,128)(2,1)} %get-tuple-element.22.early_ref), custom_call_target="tpu_custom_call" | custom-call | tf_op jit(solution)/shard_map/front_rows/pallas_call | solution.py:675
  110.4 0.0 copy-start.1
  110.4 8.3 %all-to-all-start = ((bf16[128,2,128,128]{3,2,1,0:T(8,128)(2,1)}), bf16[128,2,128,128]{3,2,1,0:T(8,128)(2,1)}, u32[]{:S(2)}, u32[]{:S(2)}) async-start(bf16[128,2,128,128]{3,2,1,0:T(8,128)(2,1)} %bitcast.105), calls=%async_computation | async-start | bytes 16777216 | tf_op jit(solution)/shard_map/all_to_all | solution.py:937
  118.7 0.0 copy-start
  118.8 0.1 select_reduce_fusion.3
  118.9 0.2 select_reduce_fusion.2
  119.1 0.1 copy.21
  119.2 0.1 reshape.207.place_ref
  119.3 0.0 copy-done.1
  119.3 0.0 copy-start.2
  119.4 0.2 copy.22
  119.6 0.2 copy.24
  119.8 0.3 abs_reduce_fusion
  120.1 0.3 copy.25
  120.5 0.1 select_add_fusion.pivot_ref
  120.6 25.0 %pivot_factor.1 = (f32[512,512]{1,0:T(8,128)S(1)}, f32[512,512]{1,0:T(8,128)S(1)}) custom-call(f32[512,512]{1,0:T(8,128)S(1)} %select_add_fusion.pivot_ref), custom_call_target="tpu_custom_call" | custom-call | tf_op jit(solution)/shard_map/pivot_factor/pallas_call | solution.py:217
  145.6 0.0 copy-done
  145.6 1.8 fusion.panel_ref
  147.5 107.5 %panel_spread.1 = (bf16[4096,512]{1,0:T(8,128)(2,1)}, bf16[512,512]{1,0:T(8,128)(2,1)}) custom-call(bf16[128,512]{1,0:T(8,128)(2,1)} %fusion.panel_ref), custom_call_target="tpu_custom_call" | custom-call | tf_op jit(solution)/shard_map/panel_spread/pallas_call | solution.py:865
  255.0 0.7 convert_reduce_fusion.2.start_ref
  255.7 0.2 convert_reduce_fusion
  255.9 0.7 select_reduce_fusion.order_ref
  256.6 0.0 all-to-all-done
  256.6 0.0 copy-done.2
  256.6 14.7 %trailing_front.1 = f32[4096,512]{1,0:T(8,128)} custom-call(s32[256]{0:T(256)} %copy-done.2, s32[256]{0:T(256)} %select_reduce_fusion.order_ref, s32[9]{0:T(128)} %convert_reduce_fusion.2.start_ref, bf16[4096,512]{1,0:T(8,128)(2,1)} %get-tuple-element.29.row_ref, bf16[512,512]{1,0:T(8,128)(2,1)} %get-tuple-element.30.col_ref, bf16[4096,512]{1,0:T(8,128)(2,1)} %base_ref.3, ...), custom_call_target="tpu_custom_call" | custom-call | tf_op jit(solution)/shard_map/trailing_front/pallas_call | solution.py:275
  (10 shorter events, 0.1 us)
Async XLA Ops:
  110.4 8.9 %copy-start.1 = (bf16[512,512]{1,0:T(8,128)(2,1)S(1)}, bf16[512,512]{1,0:T(8,128)(2,1)}, u32[]{:S(2)}) copy-start(bf16[512,512]{1,0:T(8,128)(2,1)} %get-tuple-element.25) | copy-start | bytes 1572868
  110.4 146.2 %all-to-all-start = ((bf16[128,2,128,128]{3,2,1,0:T(8,128)(2,1)}), bf16[128,2,128,128]{3,2,1,0:T(8,128)(2,1)}, u32[]{:S(2)}, u32[]{:S(2)}) async-start(bf16[128,2,128,128]{3,2,1,0:T(8,128)(2,1)} %bitcast.105), calls=%async_computation | async-start | bytes 16777216 | tf_op jit(solution)/shard_map/all_to_all | solution.py:937
  118.7 26.9 %copy-start = (f32[128,512]{1,0:T(8,128)S(1)}, f32[128,512]{1,0:T(8,128)}, u32[]{:S(2)}) copy-start(f32[128,512]{1,0:T(8,128)} %front_rows.1) | copy-start | bytes 786436
  119.3 137.3 %copy-start.2 = (s32[256]{0:T(256)}, s32[256]{0:T(256)S(1)}, u32[]{:S(2)}) copy-start(s32[256]{0:T(256)S(1)} %reshape.207.place_ref) | copy-start | bytes 3076
